TPU v7x, 256 devices: a whole 4x4x8 slice. The times are simulated.
256 devices in a mesh: wide: 32 (over z_lo, x, core), depth: 8 (over z_hi, y).
Axes of the slice: x: 4, y: 4, z: 8 (z_hi: 2, z_lo: 4; z = z_hi * 4 + z_lo), core: 2. Of those that a mesh axis runs over, the one named last changes fastest.
Arguments:
- attn_out: bfloat16 [8192, 4096], P('wide', 'depth'), may hold values from -6 to 6
- resid: bfloat16 [8192, 4096], P('wide'), may hold values from -6 to 6
- out_proj: bfloat16 [4096, 4096], P('wide', 'depth'), may hold values from -0.09375 to 0.09375
- section_in: bfloat16 [8, 4096, 1024], P('depth', 'wide'), may hold values from -0.09375 to 0.09375
- codebook: bfloat16 [8, 2048, 1024], P('depth'), may hold values from -6 to 6
- decays: float32 [8, 1024], P('depth'), may hold values from 0.001 to 1
- section_out: bfloat16 [8, 1024, 2048], P('depth'), may hold values from -16 to 16
- codes: int32 [8, 8192], P(None, 'wide'), may hold values from 0 to 2047
Outputs:
- losses: float32 [8, 8192], P('depth', 'wide')
- grad_out_proj: bfloat16 [4096, 4096], P('wide', 'depth')
All inputs are finite; a program needn't handle non-finite values.
Results may differ from a plain program's by a relative error of at most 0.03.
Values may be sent and summed in bfloat16 or wider, within the bound.
A program may use at most 128 MiB of HBM per device.

v0:
```python
import jax
import jax.numpy as jnp
from jax import lax
from jax.sharding import PartitionSpec as P

LENGTH = 256


epsilon = 1e-06


def carried_in(value, axis, join, neutral, backward):
    count, mine = (lax.axis_size(axis), lax.axis_index(axis))
    pieces = jax.tree.map(lambda part: lax.all_gather(part, axis), value)
    if backward:
        pieces = jax.tree.map(lambda part: part[::-1], pieces)
        mine = count - 1 - mine
    total = jax.tree.map(
        lambda part, zero: jnp.full_like(part, 0) + jnp.asarray(zero, part.dtype), value, neutral
    )

    def hop(position, total):
        longer = join(total, jax.tree.map(lambda part: part[position], pieces))
        return jax.tree.map(lambda new, old: jnp.where(position < mine, new, old), longer, total)

    return lax.fori_loop(0, count - 1, hop, total)


def inverse_rms(values):
    return lax.rsqrt(jnp.mean(values * values, axis=-1, keepdims=True) + epsilon)


def rms_backward(values, upstream):
    factor = inverse_rms(values)
    inner = jnp.mean(upstream * values, axis=-1, keepdims=True)
    return factor * upstream - values * (factor * factor * factor) * inner


def previous_codes(codes):
    shifted = jnp.concatenate([jnp.zeros((1,), jnp.int32), codes[-1, :-1]])
    return jnp.concatenate([shifted[None, :], codes[:-1]], axis=0)


def chain_step(earlier, latter):
    return (earlier[0] * latter[0], latter[0] * earlier[1] + latter[1])


def local(attn_out, resid, out_proj, section_in, codebook, decays, section_out, codes):
    frame_count = attn_out.shape[0]
    local_count = codebook.shape[0]
    code_count = codebook.shape[1]
    inner_width = codebook.shape[2]
    depth_count = lax.axis_size("depth")
    depth_rank = lax.axis_index("depth")
    row_share = frame_count // depth_count
    partial_mix = lax.dot_general(
        attn_out,
        lax.all_gather(out_proj, "wide", axis=0, tiled=True),
        (((1,), (1,)), ((), ())),
        preferred_element_type=jnp.float32,
    )
    mixed_rows = lax.psum_scatter(partial_mix, "depth", scatter_dimension=0, tiled=True)
    resid_rows = lax.dynamic_slice_in_dim(resid, depth_rank * row_share, row_share, 0)
    pre_part = resid_rows.astype(jnp.float32) + mixed_rows
    normed_part = (pre_part * inverse_rms(pre_part)).astype(jnp.bfloat16)
    context = lax.all_gather(normed_part, "depth", axis=0, tiled=True)
    section_full = lax.all_gather(section_in, "wide", axis=1, tiled=True)
    projected = jnp.einsum("rd,sde->sre", context, section_full, preferred_element_type=jnp.float32)
    previous = previous_codes(codes)
    positions = jnp.arange(frame_count, dtype=jnp.int32) % LENGTH
    columns = jnp.arange(code_count, dtype=jnp.int32)
    section_base = depth_rank * local_count
    offset = 0
    section_index = section_base + offset
    code_ids = lax.dynamic_index_in_dim(previous, section_index, 0, keepdims=False)
    keep_mask = jnp.logical_or(section_index != 0, positions != 0).astype(jnp.float32)[:, None]
    embedded = jnp.take(codebook[offset], code_ids, axis=0).astype(jnp.float32) * keep_mask
    inputs = [projected[offset] + embedded]
    decay_all = jnp.ones((inner_width,), jnp.float32)
    sum_all = jnp.zeros((frame_count, inner_width), jnp.float32)
    offset = 0
    decay_all = decays[offset] * decay_all
    sum_all = decays[offset] * sum_all + inputs[offset]
    identity = (
        jnp.ones((inner_width,), jnp.float32),
        jnp.zeros((frame_count, inner_width), jnp.float32),
    )
    entering = carried_in((decay_all, sum_all), "depth", chain_step, identity, False)[1]
    state = entering
    offset = 0
    section_index = section_base + offset
    state = decays[offset] * state + inputs[offset]
    normed = (state * inverse_rms(state)).astype(jnp.bfloat16)
    logits = jnp.dot(normed, section_out[offset], preferred_element_type=jnp.float32)
    total_log = jax.nn.logsumexp(logits, axis=1)
    targets = lax.dynamic_index_in_dim(codes, section_index, 0, keepdims=False)
    chosen = columns[None, :] == targets[:, None]
    picked = jnp.sum(jnp.where(chosen, logits, 0.0), axis=1)
    loss_rows = [total_log - picked]
    probs = jnp.exp(logits - total_log[:, None])
    dlogits = (probs - chosen.astype(jnp.float32)).astype(jnp.bfloat16)
    grad_normed = lax.dot_general(
        dlogits, section_out[offset], (((1,), (1,)), ((), ())), preferred_element_type=jnp.float32
    )
    local_grads = [rms_backward(state, grad_normed)]
    decay_back = jnp.ones((inner_width,), jnp.float32)
    sum_back = jnp.zeros((frame_count, inner_width), jnp.float32)
    for offset in reversed(range(local_count)):
        sum_back = decays[offset] * (local_grads[offset] + sum_back)
        decay_back = decays[offset] * decay_back
    arriving = carried_in((decay_back, sum_back), "depth", chain_step, identity, True)[1]
    carried = arriving
    carried_parts = [None] * local_count
    for offset in reversed(range(local_count)):
        grad_here = local_grads[offset] + carried
        carried_parts[offset] = grad_here.astype(jnp.bfloat16)
        carried = decays[offset] * grad_here
    carried_half = jnp.stack(carried_parts)
    context_term = jnp.einsum(
        "sre,sde->rd", carried_half, section_full, preferred_element_type=jnp.float32
    )
    context_rows = lax.psum_scatter(context_term, "depth", scatter_dimension=0, tiled=True)
    grad_part = rms_backward(pre_part, context_rows).astype(jnp.bfloat16)
    grad_pre = lax.all_gather(grad_part, "depth", axis=0, tiled=True)
    grad_local = lax.psum_scatter(
        lax.dot_general(
            grad_pre, attn_out, (((0,), (0,)), ((), ())), preferred_element_type=jnp.float32
        ).astype(jnp.bfloat16),
        "wide",
        scatter_dimension=0,
        tiled=True,
    )
    return (jnp.stack(loss_rows), grad_local)


def solution(mesh):
    return jax.shard_map(
        local,
        mesh=mesh,
        in_specs=(
            P("wide", "depth"),
            P("wide", None),
            P("wide", "depth"),
            P("depth", "wide", None),
            P("depth", None, None),
            P("depth", None),
            P("depth", None, None),
            P(None, "wide"),
        ),
        out_specs=(P("depth", "wide"), P("wide", "depth")),
        check_vma=False,
    )
```

profile of v0, /device:TPU:27, one launch (start us, length us, event | category | flops | bytes accessed | tf_op | source)
XLA Modules:
  0.0 1094.3 jit_solution(15520198171391963346)
XLA Ops:
  8.0 67.7 %all-gather.9.cloned.1.call-done = bf16[4096,512]{1,0:T(8,128)(2,1)} async-done(((bf16[128,512]{1,0:T(8,128)(2,1)}), bf16[4096,512]{1,0:T(8,128)(2,1)}) %all-gather.9.cloned.1.call-update) | async-done | bytes 4194320 | tf_op jit(solution)/shard_map/all_gather | solution.py:58
  75.6 5.4 fusion.20
  81.9 122.1 %reduce-scatter.4.cloned.1.call-done = f32[32,4096]{1,0:T(8,128)} async-done(((f32[256,4096]{1,0:T(8,128)}), f32[32,4096]{1,0:T(8,128)}) %reduce-scatter.4.cloned.1.call-update) | async-done | bytes 524304 | tf_op jit(solution)/shard_map/reduce_scatter | solution.py:62
  207.4 4.3 gather_fusion
  211.8 61.6 %all-gather.13.cloned.1.call-done = bf16[1,4096,1024]{2,1,0:T(8,128)(2,1)} async-done(((bf16[1,128,1024]{2,1,0:T(8,128)(2,1)}), bf16[1,4096,1024]{2,1,0:T(8,128)(2,1)}) %all-gather.13.cloned.1.call-update) | async-done | bytes 8388624 | tf_op jit(solution)/shard_map/all_gather | solution.py:67
  273.4 74.9 %all-gather.11.cloned.1.call-done = bf16[256,4096]{1,0:T(8,128)(2,1)} async-done(((bf16[32,4096]{1,0:T(8,128)(2,1)}), bf16[256,4096]{1,0:T(8,128)(2,1)}) %all-gather.11.cloned.1.call-update) | async-done | bytes 2097168 | tf_op jit(solution)/shard_map/all_gather | solution.py:66
  348.3 7.7 fusion.10
  356.1 40.8 %all-gather.1 = f32[8,1,1024]{2,1,0:T(1,128)S(1)} all-gather(f32[1,1,1024]{2,1,0:T(1,128)S(1)} %bitcast.75), channel_id=1, replica_groups=mesh['wide'=32,'depth'=8] {'depth'}, dimensions={0}, use_global_device_ids=true | all-gather | bytes 36864 | tf_op jit(solution)/shard_map/all_gather | solution.py:14
  396.9 128.5 %all-gather.15.cloned.1.call-done = f32[8,256,1024]{2,1,0:T(8,128)} async-done(((f32[1,256,1024]{2,1,0:T(8,128)}), f32[8,256,1024]{2,1,0:T(8,128)}) %all-gather.15.cloned.1.call-update) | async-done | bytes 8388624 | tf_op jit(solution)/shard_map/all_gather | solution.py:14
  525.3 15.2 %while.28 = (s32[]{:T(128)}, f32[256,1024]{1,0:T(8,128)S(1)}, s32[]{:T(128)}, f32[8,1024]{1,0:T(8,128)S(1)}, f32[8,256,1024]{2,1,0:T(8,128)}, /*index=5*/s32[]{:T(128)}, s32[]{:T(128)}) while((s32[]{:T(128)}, f32[256,1024]{1,0:T(8,128)S(1)}, s32[]{:T(128)}, f32[8,1024]{1,0:T(8,128)S(1)}, f32[8,256,1024]{2,1,0:T(8,128)}, ...), condition=%wide.region_3.4_spmd.clone, body=%wide.region_2.3_spmd.clone.sunk | while | flops 1048580 | bytes 3158121 | solution.py:26
  527.5 2.1 fusion.28
  529.7 2.1 fusion.28
  531.9 2.1 fusion.28
  534.1 2.1 fusion.28
  536.2 2.1 fusion.28
  538.4 2.1 fusion.28
  542.2 3.7 fusion.19
  549.9 167.8 %all-gather.19.cloned.1.call-done = f32[2048,1024]{1,0:T(8,128)} async-done(((f32[256,1024]{1,0:T(8,128)}), f32[2048,1024]{1,0:T(8,128)}) %all-gather.19.cloned.1.call-update) | async-done | bytes 8388624 | tf_op jit(solution)/shard_map/all_gather | solution.py:14
  717.7 8.3 rev.7
  726.0 15.2 %while.29 = (s32[]{:T(128)}, f32[256,1024]{1,0:T(8,128)S(1)}, s32[]{:T(128)}, f32[8,1024]{1,0:T(8,128)S(1)}, f32[8,256,1024]{2,1,0:T(8,128)}, /*index=5*/s32[]{:T(128)}, s32[]{:T(128)}) while((s32[]{:T(128)}, f32[256,1024]{1,0:T(8,128)S(1)}, s32[]{:T(128)}, f32[8,1024]{1,0:T(8,128)S(1)}, f32[8,256,1024]{2,1,0:T(8,128)}, ...), condition=%wide.region_10.11_spmd.clone, body=%wide.region_9.10_spmd.clone.sunk | while | flops 1048580 | bytes 3158121 | solution.py:26
  726.0 2.1 fusion.29
  728.2 2.1 fusion.29
  730.3 2.1 fusion.29
  732.5 2.1 fusion.29
  734.7 2.1 fusion.29
  736.9 2.1 fusion.29
  739.1 2.1 fusion.29
  741.2 7.8 fusion.2
  749.1 121.3 %reduce-scatter.6.cloned.1.call-done = f32[32,4096]{1,0:T(8,128)} async-done(((f32[256,4096]{1,0:T(8,128)}), f32[32,4096]{1,0:T(8,128)}) %reduce-scatter.6.cloned.1.call-update) | async-done | bytes 524304 | tf_op jit(solution)/shard_map/reduce_scatter | solution.py:122
  873.7 72.1 %all-gather.17.cloned.1.call-done = bf16[256,4096]{1,0:T(8,128)(2,1)} async-done(((bf16[32,4096]{1,0:T(8,128)(2,1)}), bf16[256,4096]{1,0:T(8,128)(2,1)}) %all-gather.17.cloned.1.call-update) | async-done | bytes 2097168 | tf_op jit(solution)/shard_map/all_gather | solution.py:124
  945.8 4.8 convolution_convert_fusion
  951.2 136.6 %reduce-scatter.8.cloned.1.call-done = bf16[128,512]{1,0:T(8,128)(2,1)} async-done(((bf16[4096,512]{1,0:T(8,128)(2,1)}), bf16[128,512]{1,0:T(8,128)(2,1)}) %reduce-scatter.8.cloned.1.call-update) | async-done | bytes 131088 | tf_op jit(solution)/shard_map/reduce_scatter | solution.py:125
  (69 shorter events, 16.8 us)
Async XLA Ops:
  7.2 68.5 %copy-start = (bf16[256,512]{1,0:T(8,128)(2,1)S(1)}, bf16[256,512]{1,0:T(8,128)(2,1)}, u32[]{:S(2)}) copy-start(bf16[256,512]{1,0:T(8,128)(2,1)} %param.12) | copy-start | bytes 786436
  7.2 68.5 %all-gather.9.cloned.1.call-start = ((), (), s32[]{:S(2)}) async-start(), calls=%async_computation.3 | async-start | bytes 4325376 | tf_op jit(solution)/shard_map/all_gather | solution.py:58
  7.9 196.1 %reduce-scatter.4.cloned.1.call-start = ((), (), s32[]{:S(2)}) async-start(), calls=%async_computation.4 | async-start | bytes 4718592 | tf_op jit(solution)/shard_map/reduce_scatter | solution.py:62
  81.1 126.2 %copy-start.4 = (s32[8,256]{1,0:T(8,128)S(1)}, s32[8,256]{1,0:T(8,128)}, u32[]{:S(2)}) copy-start(s32[8,256]{1,0:T(8,128)} %param.19) | copy-start | bytes 24580
  81.1 130.6 %copy-start.3 = (f32[1,1024]{1,0:T(1,128)S(1)}, f32[1,1024]{1,0:T(1,128)}, u32[]{:S(2)}) copy-start(f32[1,1024]{1,0:T(1,128)} %param.17) | copy-start | bytes 12292
  81.1 192.3 %all-gather.13.cloned.1.call-start = ((), (), s32[]{:S(2)}) async-start(), calls=%async_computation.6 | async-start | bytes 8650752 | tf_op jit(solution)/shard_map/all_gather | solution.py:67
  81.9 266.4 %all-gather.11.cloned.1.call-start = ((), (), s32[]{:S(2)}) async-start(), calls=%async_computation.5 | async-start | bytes 2359296 | tf_op jit(solution)/shard_map/all_gather | solution.py:66
  207.2 318.1 %all-gather.15.cloned.1.call-start = ((), (), s32[]{:S(2)}) async-start(), calls=%async_computation.7 | async-start | bytes 9437184 | tf_op jit(solution)/shard_map/all_gather | solution.py:14
  356.0 361.7 %all-gather.19.cloned.1.call-start = ((), (), s32[]{:S(2)}) async-start(), calls=%async_computation.11 | async-start | bytes 9437184 | tf_op jit(solution)/shard_map/all_gather | solution.py:14
  542.2 4.4 copy-start.2
  549.5 320.8 %reduce-scatter.6.cloned.1.call-start = ((), (), s32[]{:S(2)}) async-start(), calls=%async_computation.8 | async-start | bytes 4718592 | tf_op jit(solution)/shard_map/reduce_scatter | solution.py:122
  749.0 121.3 %copy-start.1 = (f32[32,4096]{1,0:T(8,128)S(1)}, f32[32,4096]{1,0:T(8,128)}, u32[]{:S(2)}) copy-start(f32[32,4096]{1,0:T(8,128)} %reduce-scatter.4.cloned.1.call-done) | copy-start | bytes 1572868
  749.0 196.7 %all-gather.17.cloned.1.call-start = ((), (), s32[]{:S(2)}) async-start(), calls=%async_computation.9 | async-start | bytes 2359296 | tf_op jit(solution)/shard_map/all_gather | solution.py:124
  873.6 214.1 %reduce-scatter.8.cloned.1.call-start = ((), (), s32[]{:S(2)}) async-start(), calls=%async_computation.10 | async-start | bytes 4325376 | tf_op jit(solution)/shard_map/reduce_scatter | solution.py:125
Sparse Core Ops, SparseCore 0:
  9.9 65.7 all-gather.8
  81.2 122.7 reduce-scatter.3
  205.8 67.4 all-gather.12
  275.9 72.3 all-gather.10
  356.1 169.1 all-gather.14
  549.6 168.0 all-gather.18
  749.2 121.1 reduce-scatter.5
  873.8 71.9 all-gather.16
  950.7 136.9 reduce-scatter.7
where the time goes:
time: 1110 us; the launch traced here: 1090 us
  waiting for transfers between devices  954 us (86%)
  other arithmetic  40.8 us (4%)
  blocking collectives  40.8 us (4%)
  matrix products  31 us (3%)
  between operations  14 us (1%)
  local copies, waits for them, and re-layouts  12.9 us (1%)
    all_gather x2, waiting for transfers between devices, carried_in(): pieces = jax.tree.map(lambda part: lax.all_gather(part, axis), value)  296 us
    reduce_scatter x1, waiting for transfers between devices, local(): lax.psum_scatter(lax.dot_general(grad_pre, attn_out, (((0,), (0,)), ((),...  137 us
    reduce_scatter x1, waiting for transfers between devices, local(): lax.psum_scatter(partial_mix, 'depth', scatter_dimension=0, tiled=True)  122 us
    reduce_scatter x1, waiting for transfers between devices, local(): lax.psum_scatter(context_term, 'depth', scatter_dimension=0, tiled=True)  121 us
    all_gather x1, waiting for transfers between devices, local(): context = lax.all_gather(normed_part, 'depth', axis=0, tiled=True)  74.9 us
    all_gather x1, waiting for transfers between devices, local(): grad_pre = lax.all_gather(grad_part, 'depth', axis=0, tiled=True)  72.1 us
    all_gather x1, waiting for transfers between devices, local(): lax.all_gather(out_proj, 'wide', axis=0, tiled=True)  67.7 us
    all_gather x1, waiting for transfers between devices, local(): section_full = lax.all_gather(section_in, 'wide', axis=1, tiled=True)  61.6 us
  transfers between devices with their start and end apart: 9, of which 9 were waited for; matrix products, arithmetic and copies ran while one was open for 1% of the time, Pallas kernels for 0%

commit v1 on v0

v1 whole, which is shorter than its diff:
```python
import functools

import jax
import jax.numpy as jnp
from jax import lax
from jax.experimental import pallas as pl
from jax.experimental.pallas import tpu as pltpu
from jax.sharding import PartitionSpec as P

MESH = pl.DeviceIdType.MESH
LENGTH = 256
EPSILON = 1e-06
BF = jnp.bfloat16
F32 = jnp.float32
VMEM_LIMIT = 50 << 20
NT = (((1,), (1,)), ((), ()))


class Place:
    def __init__(self):
        w, d = lax.axis_index("wide"), lax.axis_index("depth")
        self.zl, self.x, self.c = w // 8, (w // 2) % 4, w % 2
        self.zh, self.y = d // 4, d % 4
        self.d = d

    def at(self, zl=None, x=None, c=None, zh=None, y=None):
        zl = self.zl if zl is None else zl
        x = self.x if x is None else x
        c = self.c if c is None else c
        zh = self.zh if zh is None else zh
        y = self.y if y is None else y
        return (zl * 8 + x * 2 + c, zh * 4 + y)

    def ys(self):
        return [(self.y + k) % 4 for k in (2, 1, 3)]

    def xs(self):
        return [(self.x + k) % 4 for k in (2, 1, 3)]

    def zls(self):
        return [(self.zl + k) % 4 for k in (2, 1, 3)]

    def to_features(self):
        return self.at(
            zh=self.zl // 2,
            y=(self.zl % 2) * 2 + self.x // 2,
            zl=(self.x % 2) * 2 + self.zh,
            x=self.y,
            c=1 - self.c,
        )

    def to_owner(self):
        return self.at(
            zl=self.zh * 2 + self.y // 2,
            x=(self.y % 2) * 2 + self.zl // 2,
            c=1 - self.c,
            zh=self.zl % 2,
            y=self.x,
        )


class Copies:
    def __init__(self, send_sem, recv_sem):
        self.send_sem, self.recv_sem = send_sem, recv_sem
        self.used = 0
        self.sent = []

    def send(self, source, target, device):
        copy = pltpu.make_async_remote_copy(
            src_ref=source,
            dst_ref=target,
            send_sem=self.send_sem.at[self.used],
            recv_sem=self.recv_sem.at[self.used],
            device_id=device,
            device_id_type=MESH,
        )
        self.used += 1
        copy.start()
        self.sent.append(copy)
        return copy

    def finish(self):
        for copy in self.sent:
            copy.wait_send()


def greet(senders, targets):
    barrier = pltpu.get_barrier_semaphore()
    for device in senders:
        pl.semaphore_signal(barrier, inc=1, device_id=device, device_id_type=MESH)
    pl.semaphore_wait(barrier, len(targets))


def columns(d, width):
    return pl.ds(pl.multiple_of(d * width, width), width)


def front_kernel(
    attn_ref, resid_ref, proj_ref, sec_ref, dec_ref,
    pre_ref, mine_ref, sect_ref, full_ref, decs_ref,
    wd, resid_part, send_sem, recv_sem, local_sem,
):
    me = Place()
    copies = Copies(send_sem, recv_sem)
    width = attn_ref.shape[1]
    own = columns(me.d, width)
    across = columns((1 - me.zh) * 4 + me.y, width)
    resid_copy = pltpu.make_async_copy(resid_ref.at[:, own], resid_part, local_sem.at[0])
    resid_copy.start()
    decs_ref[me.y] = jnp.broadcast_to(dec_ref[...], decs_ref.shape[1:])
    sect_ref[me.zl, me.x, me.c] = sec_ref[...]
    full_ref[:, own] = attn_ref[...]
    y_peers = [me.at(y=y) for y in me.ys()]
    zl_peers = [me.at(zl=zl) for zl in me.zls()]
    right, left = me.at(x=(me.x + 1) % 4), me.at(x=(me.x + 3) % 4)
    far, other = me.at(zh=1 - me.zh), me.at(c=1 - me.c)
    shared = y_peers + zl_peers + [right, left, far, other]
    greet(shared + [me.to_owner()], shared + [me.to_features()])

    dest = me.to_features()
    f_zl, f_x, f_c = dest[0] // 8, (dest[0] // 2) % 4, dest[0] % 2
    moved = copies.send(proj_ref, wd.at[f_zl, f_x, f_c], dest)
    attn_far = copies.send(attn_ref, full_ref.at[:, own], far)
    attn_near = [copies.send(attn_ref, full_ref.at[:, own], peer) for peer in y_peers]
    dec_near = [copies.send(decs_ref.at[me.y], decs_ref.at[me.y], peer) for peer in y_peers]

    moved.wait_recv()
    mine_wd = wd.at[me.zl, me.x, me.c]
    wd_z = [copies.send(mine_wd, mine_wd, peer) for peer in zl_peers]
    sec_slot = sect_ref.at[me.zl, me.x, me.c]
    sec_z = [copies.send(sec_ref, sec_slot, peer) for peer in zl_peers]
    attn_far.wait_recv()
    attn_far_near = [copies.send(full_ref.at[:, across], full_ref.at[:, across], peer) for peer in y_peers]

    def ring_first(buffer):
        group = buffer.at[:, me.x, me.c]
        to_right = copies.send(group, group, right)
        to_left = copies.send(group, group, left)
        to_other = copies.send(group, group, other)
        return to_right, to_left, to_other

    def ring_second(buffer, to_right, to_left):
        to_right.wait_recv()
        from_left = (me.x + 3) % 4
        half = buffer.at[pl.ds(0, 2), from_left, me.c]
        on_right = copies.send(half, half, right)
        group = buffer.at[:, from_left, me.c]
        other_a = copies.send(group, group, other)
        to_left.wait_recv()
        from_right = (me.x + 1) % 4
        half = buffer.at[pl.ds(2, 2), from_right, me.c]
        on_left = copies.send(half, half, left)
        group = buffer.at[:, from_right, me.c]
        other_b = copies.send(group, group, other)
        return on_right, on_left, other_a, other_b

    def ring_third(buffer, on_right, on_left):
        on_right.wait_recv()
        on_left.wait_recv()
        group = buffer.at[:, (me.x + 2) % 4, me.c]
        return copies.send(group, group, other)

    for copy in wd_z:
        copy.wait_recv()
    w1 = ring_first(wd)
    w2 = ring_second(wd, w1[0], w1[1])
    for copy in sec_z:
        copy.wait_recv()
    s1 = ring_first(sect_ref)
    w3 = ring_third(wd, w2[0], w2[1])
    for copy in [w1[2], w2[2], w2[3], w3] + attn_near + attn_far_near:
        copy.wait_recv()
    resid_copy.wait()

    block = proj_ref.shape[0]
    for u in range(2):
        total = jnp.zeros((attn_ref.shape[0], 2 * block), F32)
        for head in range(8):
            weight = wd[u * 2 + head // 4, head % 4].reshape(2 * block, width)
            total += lax.dot_general(
                full_ref[:, head * width : (head + 1) * width], weight, NT, preferred_element_type=F32
            )
        for c in range(2):
            feature = (2 * u + 1 - c) * block
            part = resid_part[:, feature : feature + block].astype(F32) + total[:, c * block : (c + 1) * block]
            mine_ref[:, feature : feature + block] = part.astype(BF)
    pre_ref[:, own] = mine_ref[...]

    pre_far = copies.send(mine_ref, pre_ref.at[:, own], far)
    pre_near = [copies.send(mine_ref, pre_ref.at[:, own], peer) for peer in y_peers]
    s2 = ring_second(sect_ref, s1[0], s1[1])
    pre_far.wait_recv()
    pre_far_near = [copies.send(pre_ref.at[:, across], pre_ref.at[:, across], peer) for peer in y_peers]
    s3 = ring_third(sect_ref, s2[0], s2[1])
    for copy in pre_near + pre_far_near + dec_near + [s1[2], s2[2], s2[3], s3]:
        copy.wait_recv()
    copies.finish()


def front(attn_out, resid, out_proj, section_in, decays):
    frames, width = attn_out.shape
    block, inner = section_in.shape
    vmem = pl.BlockSpec(memory_space=pltpu.VMEM)
    return pl.pallas_call(
        front_kernel,
        out_shape=(
            jax.ShapeDtypeStruct((frames, 8 * width), BF),
            jax.ShapeDtypeStruct((frames, width), BF),
            jax.ShapeDtypeStruct((4, 4, 2, block, inner), BF),
            jax.ShapeDtypeStruct((frames, 8 * width), BF),
            jax.ShapeDtypeStruct((4, 8, inner), F32),
        ),
        in_specs=[vmem, pl.BlockSpec(memory_space=pl.ANY), vmem, vmem, vmem],
        out_specs=[vmem] * 5,
        scratch_shapes=[
            pltpu.VMEM((4, 4, 2) + out_proj.shape, BF),
            pltpu.VMEM((frames, width), BF),
            pltpu.SemaphoreType.DMA((48,)),
            pltpu.SemaphoreType.DMA((48,)),
            pltpu.SemaphoreType.DMA((1,)),
        ],
        compiler_params=pltpu.CompilerParams(
            collective_id=0, has_side_effects=True, vmem_limit_bytes=VMEM_LIMIT
        ),
        name="front",
    )(attn_out, resid, out_proj, section_in, decays)


def scan_kernel(
    backward, in_ref, dec_ref, out_ref, got, done, carry_in, carry_out, send_sem, recv_sem, carry_send, carry_recv
):
    me = Place()
    copies = Copies(send_sem, recv_sem)
    rows = got.shape[1]
    carry_in[...] = jnp.zeros_like(carry_in)
    y_peers = [me.at(y=y) for y in me.ys()]
    far = me.at(zh=1 - me.zh)
    greet(y_peers + [far], y_peers + [far])
    first = 1 if backward else 0

    def part(y):
        return pl.ds(pl.multiple_of(y * rows, rows), rows)

    there = [copies.send(in_ref.at[part(y)], got.at[me.y], me.at(y=y)) for y in me.ys()]
    got[me.y] = in_ref[part(me.y)]
    for copy in there:
        copy.wait_recv()
    carry = pltpu.make_async_remote_copy(
        src_ref=carry_out,
        dst_ref=carry_in,
        send_sem=carry_send.at[0],
        recv_sem=carry_recv.at[0],
        device_id=far,
        device_id_type=MESH,
    )

    @pl.when(me.zh != first)
    def _():
        carry.wait_recv()

    state = carry_in[...].astype(F32)
    for section in reversed(range(4)) if backward else range(4):
        decay = dec_ref[section, 0:1]
        if backward:
            here = got[section].astype(F32) + state
            done[section] = here.astype(BF)
            state = decay * here
        else:
            state = decay * state + got[section].astype(F32)
            done[section] = state.astype(BF)
    carry_out[...] = state.astype(BF)

    @pl.when(me.zh == first)
    def _():
        carry.start()

    back = [copies.send(done.at[y], out_ref.at[part(me.y)], me.at(y=y)) for y in me.ys()]
    out_ref[part(me.y)] = done[me.y]
    for copy in back:
        copy.wait_recv()
    copies.finish()

    @pl.when(me.zh == first)
    def _():
        carry.wait_send()


def scan(backward, values, decays):
    frames, inner = values.shape
    vmem = pl.BlockSpec(memory_space=pltpu.VMEM)
    rows = frames // 4
    return pl.pallas_call(
        functools.partial(scan_kernel, backward),
        out_shape=jax.ShapeDtypeStruct((frames, inner), BF),
        in_specs=[vmem] * 2,
        out_specs=vmem,
        scratch_shapes=[
            pltpu.VMEM((4, rows, inner), BF),
            pltpu.VMEM((4, rows, inner), BF),
            pltpu.VMEM((rows, inner), BF),
            pltpu.VMEM((rows, inner), BF),
            pltpu.SemaphoreType.DMA((6,)),
            pltpu.SemaphoreType.DMA((6,)),
            pltpu.SemaphoreType.DMA((1,)),
            pltpu.SemaphoreType.DMA((1,)),
        ],
        compiler_params=pltpu.CompilerParams(
            collective_id=2 if backward else 1, has_side_effects=True, vmem_limit_bytes=VMEM_LIMIT
        ),
        name="scan_back" if backward else "scan",
    )(values, decays)


def back_kernel(
    grad_ref, inner_ref, mine_ref, factor_ref, full_ref, out_ref,
    got, far_out, far_in, inners, gp, core_got, group, group_got, line, line_got, last,
    send_sem, recv_sem,
):
    me = Place()
    copies = Copies(send_sem, recv_sem)
    frames, width = mine_ref.shape
    block = out_ref.shape[0]
    y_peers = [me.at(y=y) for y in me.ys()]
    x_peers = [me.at(x=x) for x in me.xs()]
    zl_peers = [me.at(zl=zl) for zl in me.zls()]
    far, other = me.at(zh=1 - me.zh), me.at(c=1 - me.c)
    cross = [me.at(zh=1 - me.zh, y=y) for y in me.ys()]
    shared = y_peers + x_peers + zl_peers + cross + [far, other]
    greet(shared + [me.to_features()], shared + [me.to_owner()])

    inner_sent = [copies.send(inner_ref, inners.at[me.d], peer) for peer in y_peers + [far] + cross]
    inners[me.d] = inner_ref[...]

    def cols(zh, y):
        return columns(zh * 4 + y, width)

    first = [
        copies.send(grad_ref.at[:, cols(1 - me.zh, y)], got.at[0, slot], me.at(y=y))
        for slot, y in enumerate(me.ys())
    ]
    second = [
        copies.send(grad_ref.at[:, cols(me.zh, y)], got.at[1, slot], me.at(y=y)) for slot, y in enumerate(me.ys())
    ]
    total = grad_ref[:, cols(1 - me.zh, me.y)].astype(F32)
    for slot, copy in enumerate(first):
        copy.wait_recv()
        total += got[0, slot].astype(F32)
    far_out[...] = total.astype(BF)
    crossing = copies.send(far_out, far_in, far)
    total = grad_ref[:, cols(me.zh, me.y)].astype(F32)
    for slot, copy in enumerate(second):
        copy.wait_recv()
        total += got[1, slot].astype(F32)
    for copy in inner_sent:
        copy.wait_recv()
    row = jnp.sum(inners[...], axis=0)
    lanes = lax.broadcasted_iota(jnp.int32, (128, 128), 0) == lax.broadcasted_iota(jnp.int32, (128, 128), 1)
    inner = jnp.concatenate(
        [
            jnp.sum(jnp.where(lanes, jnp.broadcast_to(row[k : k + 1], (128, 128)), 0.0), axis=1, keepdims=True)
            for k in range(frames // 128)
        ],
        axis=0,
    )
    factor = factor_ref[:, 0:1]
    scale = factor * factor * factor * inner * (1.0 / (8 * width))
    crossing.wait_recv()
    total += far_in[...].astype(F32)
    dpre = (factor * total - mine_ref[...].astype(F32) * scale).astype(BF)
    turned = dpre.astype(F32).T.astype(BF)

    def product(x):
        for zl in range(4):
            u = zl // 2
            value = jnp.dot(
                turned[u * 2 * block : (u + 1) * 2 * block],
                full_ref[:, columns((zl % 2) * 4 + x, width)],
                preferred_element_type=F32,
            ).astype(BF)
            gp[x, 0, zl] = value[block:]
            gp[x, 1, zl] = value[:block]
        return copies.send(gp.at[x, 1 - me.c], core_got.at[x], other)

    order = me.xs() + [me.x]
    in_core = [product(x) for x in order]
    along = []
    for slot, x in enumerate(order):
        in_core[slot].wait_recv()
        for zl in range(4):
            group[x, zl] = (gp[x, me.c, zl].astype(F32) + core_got[x, zl].astype(F32)).astype(BF)
        if slot < 3:
            along.append(copies.send(group.at[x], group_got.at[slot], me.at(x=x)))
    for copy in along:
        copy.wait_recv()
    for zl in range(4):
        value = group[me.x, zl].astype(F32)
        for slot in range(3):
            value += group_got[slot, zl].astype(F32)
        line[zl] = value.astype(BF)
    lines = [copies.send(line.at[zl], line_got.at[slot], me.at(zl=zl)) for slot, zl in enumerate(me.zls())]
    value = line[me.zl].astype(F32)
    for slot, copy in enumerate(lines):
        copy.wait_recv()
        value += line_got[slot].astype(F32)
    last[...] = value.astype(BF)
    home = copies.send(last, out_ref, me.to_owner())
    home.wait_recv()
    copies.finish()


def back(grad, inner, mine, factor, full, block):
    frames, width = mine.shape
    vmem = pl.BlockSpec(memory_space=pltpu.VMEM)
    return pl.pallas_call(
        back_kernel,
        out_shape=jax.ShapeDtypeStruct((block, width), BF),
        in_specs=[vmem] * 5,
        out_specs=vmem,
        scratch_shapes=[
            pltpu.VMEM((2, 3, frames, width), BF),
            pltpu.VMEM((frames, width), BF),
            pltpu.VMEM((frames, width), BF),
            pltpu.VMEM((8, 8, 128), F32),
            pltpu.VMEM((4, 2, 4, block, width), BF),
            pltpu.VMEM((4, 4, block, width), BF),
            pltpu.VMEM((4, 4, block, width), BF),
            pltpu.VMEM((3, 4, block, width), BF),
            pltpu.VMEM((4, block, width), BF),
            pltpu.VMEM((3, block, width), BF),
            pltpu.VMEM((block, width), BF),
            pltpu.SemaphoreType.DMA((32,)),
            pltpu.SemaphoreType.DMA((32,)),
        ],
        compiler_params=pltpu.CompilerParams(
            collective_id=3, has_side_effects=True, vmem_limit_bytes=VMEM_LIMIT
        ),
        name="back",
    )(grad, inner, mine, factor, full)


def inverse_rms(values):
    return lax.rsqrt(jnp.mean(values * values, axis=-1, keepdims=True) + EPSILON)


def previous_codes(codes):
    shifted = jnp.concatenate([jnp.zeros((1,), jnp.int32), codes[-1, :-1]])
    return jnp.concatenate([shifted[None, :], codes[:-1]], axis=0)


def local(attn_out, resid, out_proj, section_in, codebook, decays, section_out, codes):
    frame_count = attn_out.shape[0]
    depth_rank = lax.axis_index("depth")
    section_in, codebook, section_out = section_in[0], codebook[0], section_out[0]
    code_count, inner_width = codebook.shape
    pre, mine, section_full, attn_full, decs = front(attn_out, resid, out_proj, section_in, decays)
    section_full = section_full.reshape(-1, inner_width)

    factor = inverse_rms(pre.astype(F32))
    projected = jnp.dot(pre, section_full, preferred_element_type=F32)
    code_ids = lax.dynamic_index_in_dim(previous_codes(codes), depth_rank, 0, keepdims=False)
    positions = jnp.arange(frame_count, dtype=jnp.int32) % LENGTH
    keep_mask = jnp.logical_or(depth_rank != 0, positions != 0).astype(F32)[:, None]
    embedded = jnp.take(codebook, code_ids, axis=0).astype(F32) * keep_mask
    inputs = (projected * factor + embedded).astype(BF)

    states = scan(False, inputs, decs)

    normed = states.astype(F32) * inverse_rms(states.astype(F32))
    norm = inverse_rms(states.astype(F32))
    logits = jnp.dot(states, section_out, preferred_element_type=F32) * norm
    total_log = jax.nn.logsumexp(logits, axis=1)
    targets = lax.dynamic_index_in_dim(codes, depth_rank, 0, keepdims=False)
    chosen = jnp.arange(code_count, dtype=jnp.int32)[None, :] == targets[:, None]
    picked = jnp.sum(jnp.where(chosen, logits, 0.0), axis=1)
    losses = (total_log - picked)[None]
    dlogits = (jnp.exp(logits - total_log[:, None]) - chosen.astype(F32)).astype(BF)
    dnormed = lax.dot_general(dlogits, section_out, NT, preferred_element_type=F32)
    inner = jnp.sum(dlogits.astype(F32) * logits, axis=1, keepdims=True) / inner_width
    dstates = (norm * (dnormed - normed * inner)).astype(BF)

    carried = scan(True, dstates, decs)

    grad = lax.dot_general(carried, section_full, NT, preferred_element_type=F32).astype(BF)
    inner = jnp.sum(carried.astype(F32) * projected, axis=1).reshape(-1, 128)
    inner = jnp.pad(inner, ((0, 8 - inner.shape[0]), (0, 0)))
    grad_out = back(
        grad, inner, mine, jnp.broadcast_to(factor, (frame_count, 128)), attn_full, out_proj.shape[0]
    )
    return (losses, grad_out)


def solution(mesh):
    return jax.shard_map(
        local,
        mesh=mesh,
        in_specs=(
            P("wide", "depth"),
            P("wide", None),
            P("wide", "depth"),
            P("depth", "wide", None),
            P("depth", None, None),
            P("depth", None),
            P("depth", None, None),
            P(None, "wide"),
        ),
        out_specs=(P("depth", "wide"), P("wide", "depth")),
        check_vma=False,
    )
```

time: 1110 us -> 267 us (0.24); the launches traced: 1090 us -> 264 us
  waiting for transfers between devices: 954 us -> 0 us
  Pallas kernels: 0 us -> 241 us
  blocking collectives: 40.8 us -> 0 us
  other arithmetic: 40.8 us -> 3.78 us
  matrix products: 31 us -> 11.3 us
  between operations: 14 us -> 0.86 us
    all_gather x6 -> x0, waiting for transfers between devices: 572 us -> none  [the longest x2 296 us: carried_in(): pieces = jax.tree.map(lambda part: lax.all_gather(part, axis), value)]
    reduce_scatter x3 -> x0, waiting for transfers between devices: 380 us -> none  [the longest x1 137 us: local(): lax.psum_scatter(lax.dot_general(grad_pre, attn_out, (((0,), (0,)), ((),...]
    pallas_call x0 -> x4, Pallas kernels: none -> 241 us  [the longest x1 108 us: front(): pl.pallas_call(front_kernel, out_shape=(jax.ShapeDtypeStruct((frames, 8 *...]
    all_gather x1 -> x0, blocking collectives: 40.8 us -> none  [carried_in(): pieces = jax.tree.map(lambda part: lax.all_gather(part, axis), value)]
    select_n x15 -> x1, other arithmetic: 29.9 us -> 0.71 us  [local(): embedded = jnp.take(codebook, code_ids, axis=0).astype(F32) * keep_mask]
    dot_general x6 -> x4, matrix products: 31 us -> 11.3 us  [the longest x1 5.92 us: local(): projected = jnp.dot(pre, section_full, preferred_element_type=F32)]
  transfers between devices with their start and end apart: 9 -> 0, of which waited for: 9 -> 0; matrix products, arithmetic and copies ran while one was open for 1% -> 0% of each run, Pallas kernels for 0% -> 0%
where the time goes in v1:
time: 267 us; the launch traced here: 264 us
  Pallas kernels  241 us (90%)
  matrix products  11.3 us (4%)
  local copies, waits for them, and re-layouts  6.78 us (3%)
  other arithmetic  3.78 us (1%)
    pallas_call x1, Pallas kernels, front(): pl.pallas_call(front_kernel, out_shape=(jax.ShapeDtypeStruct((frames, 8 *...  108 us
    pallas_call x1, Pallas kernels, back(): pl.pallas_call(back_kernel, out_shape=jax.ShapeDtypeStruct((block, width)...  89 us
    pallas_call x2, Pallas kernels, scan(): pl.pallas_call(functools.partial(scan_kernel, backward), out_shape=jax.Sh...  44.2 us
    dot_general x1, matrix products, local(): projected = jnp.dot(pre, section_full, preferred_element_type=F32)  5.92 us

profile of v1, /device:TPU:27, one launch (start us, length us, event | category | flops | bytes accessed | tf_op | source)
XLA Modules:
  0.0 263.6 jit_solution(434969303782754372)
XLA Ops:
  0.6 0.7 slice.6
  1.3 0.1 pad_add_fusion
  1.4 0.7 compare_select_fusion
  2.2 0.0 copy-start
  2.2 0.0 copy-start.1
  2.2 0.0 copy-start.2
  2.2 0.0 copy-start.3
  2.2 4.3 %gather_fusion = bf16[256,1024]{1,0:T(8,128)(2,1)S(1)} fusion(bf16[2048,1024]{1,0:T(8,128)(2,1)} %bitcast.36, s32[1024]{0:T(1024)S(1)} %pad_clamp_fusion), kind=kCustom, calls=%fused_computation | custom fusion | bytes 1049600 | tf_op jit(solution)/shard_map/jit(_take)/gather | solution.py:463
  6.6 0.0 copy-done
  6.6 0.0 copy-done.1
  6.6 0.0 copy-done.2
  6.6 0.0 copy-done.3
  6.6 107.7 %front.1 = (bf16[256,4096]{1,0:T(8,128)(2,1)S(1)}, bf16[256,512]{1,0:T(8,128)(2,1)S(1)}, bf16[4,4,2,128,1024]{4,3,2,1,0:T(8,128)(2,1)}, bf16[256,4096]{1,0:T(8,128)(2,1)}, f32[4,8,1024]{2,1,0:T(8,128)S(1)}) custom-call(bf16[256,512]{1,0:T(8,128)(2,1)S(1)} %copy-done, bf16[256,4096]{1,0:T(8,128)(2,1)} %resid_ref.1, bf16[128,512]{1,0:T(8,128)(2,1)S(1)} %copy-done.2, ...), custom_call_target="tpu_custom_call" | custom-call | tf_op jit(solution)/shard_map/front/pallas_call | solution.py:204
  114.3 0.5 multiply_reduce_fusion
  114.8 0.0 copy-start.4
  114.8 5.9 %add_convert_fusion = (bf16[256,1024]{1,0:T(8,128)(2,1)S(1)}, f32[256,1024]{1,0:T(8,128)S(1)}) fusion(f32[256]{0:T(256)S(1)} %get-tuple-element.22, bf16[256,1024]{1,0:T(8,128)(2,1)S(1)} %gather_fusion, f32[256]{0:T(256)S(1)} %add_rsqrt_fusion.1, pred[256]{0:T(512)(128)(4,1)S(1)} %get-tuple-element.23, bf16[256,4096]{1,0:T(8,128)(2,1)S(1)} %get-tuple-element.7, ...), kind=kOutput, calls=%fused_computation.23 | convolution fusion | flops 2149056512 | bytes 12585216 | tf_op jit(solution)/shard_map/dot_general | solution.py:459
  120.7 19.5 %scan.1 = bf16[256,1024]{1,0:T(8,128)(2,1)S(1)} custom-call(bf16[256,1024]{1,0:T(8,128)(2,1)S(1)} %get-tuple-element.18.in_ref, f32[4,8,1024]{2,1,0:T(8,128)S(1)} %get-tuple-element.9.dec_ref), custom_call_target="tpu_custom_call" | custom-call | tf_op jit(solution)/shard_map/scan/pallas_call | solution.py:292
  140.2 0.2 fusion.16
  140.4 0.0 copy-done.4
  140.4 1.4 fusion.25
  141.8 0.0 slice-start
  141.8 0.4 exponential_reduce_fusion
  142.3 0.9 constant_dynamic-slice_fusion
  143.2 1.1 multiply_reduce_fusion.1
  144.3 0.6 fusion.21
  144.9 1.4 fusion.13.in_ref
  146.3 24.7 %scan_back.1 = bf16[256,1024]{1,0:T(8,128)(2,1)S(1)} custom-call(bf16[256,1024]{1,0:T(8,128)(2,1)S(1)} %fusion.13.in_ref, f32[4,8,1024]{2,1,0:T(8,128)S(1)} %get-tuple-element.9.dec_ref), custom_call_target="tpu_custom_call" | custom-call | tf_op jit(solution)/shard_map/scan_back/pallas_call | solution.py:292
  171.1 2.6 convolution_convert_fusion.grad_ref
  173.7 0.2 multiply_reduce_fusion.2
  173.8 0.1 broadcast_in_dim.43.factor_ref
  173.9 89.0 %back.1 = bf16[128,512]{1,0:T(8,128)(2,1)S(1)} custom-call(bf16[256,4096]{1,0:T(8,128)(2,1)S(1)} %convolution_convert_fusion.grad_ref, f32[8,128]{1,0:T(8,128)S(1)} %pad.4.inner_ref, bf16[256,512]{1,0:T(8,128)(2,1)S(1)} %get-tuple-element.10.mine_ref, f32[256,128]{1,0:T(8,128)S(1)} %broadcast_in_dim.43.factor_ref, bf16[256,4096]{1,0:T(8,128)(2,1)} %get-tuple-element.11.full_ref), custom_call_target="tpu_custom_call" | custom-call | tf_op jit(solution)/shard_map/back/pallas_call | solution.py:414
  262.9 0.7 copy.11
  (14 shorter events, 0.1 us)
Async XLA Ops:
  2.2 4.4 %copy-start = (bf16[256,512]{1,0:T(8,128)(2,1)S(1)}, bf16[256,512]{1,0:T(8,128)(2,1)}, u32[]{:S(2)}) copy-start(bf16[256,512]{1,0:T(8,128)(2,1)} %attn_ref.1) | copy-start | bytes 786436
  2.2 4.4 %copy-start.1 = (bf16[1,128,1024]{2,1,0:T(8,128)(2,1)S(1)}, bf16[1,128,1024]{2,1,0:T(8,128)(2,1)}, u32[]{:S(2)}) copy-start(bf16[1,128,1024]{2,1,0:T(8,128)(2,1)} %param.11) | copy-start | bytes 786436
  2.2 4.4 %copy-start.2 = (bf16[128,512]{1,0:T(8,128)(2,1)S(1)}, bf16[128,512]{1,0:T(8,128)(2,1)}, u32[]{:S(2)}) copy-start(bf16[128,512]{1,0:T(8,128)(2,1)} %proj_ref.1) | copy-start | bytes 393220
  2.2 4.4 %copy-start.3 = (f32[1,1024]{1,0:T(1,128)S(1)}, f32[1,1024]{1,0:T(1,128)}, u32[]{:S(2)}) copy-start(f32[1,1024]{1,0:T(1,128)} %dec_ref.1) | copy-start | bytes 12292
  114.8 25.6 %copy-start.4 = (bf16[1,1024,2048]{2,1,0:T(8,128)(2,1)S(1)}, bf16[1,1024,2048]{2,1,0:T(8,128)(2,1)}, u32[]{:S(2)}) copy-start(bf16[1,1024,2048]{2,1,0:T(8,128)(2,1)} %param.14) | copy-start | bytes 12582916
  141.8 3.1 %copy-start.5 = (bf16[1,1024,2048]{2,1,0:T(8,128)(2,1)S(1)}, bf16[1,1024,2048]{2,1,0:T(8,128)(2,1)}, u32[]{:S(2)}) copy-start(bf16[1,1024,2048]{2,1,0:T(8,128)(2,1)} %param.14) | copy-start | bytes 12582916
  141.8 29.2 %slice-start = ((s8[8388608]{0:T(1024)(128)(4,1)}), s8[4194304]{0:T(1024)(128)(4,1)S(1)}, s32[]{:S(2)}) async-start(s8[8388608]{0:T(1024)(128)(4,1)} %bitcast.49), calls=%async_computation | async-start | bytes 8388608
  144.9 26.1 %slice-start.1 = ((s8[8388608]{0:T(1024)(128)(4,1)}), s8[4194304]{0:T(1024)(128)(4,1)S(1)}, s32[]{:S(2)}) async-start(s8[8388608]{0:T(1024)(128)(4,1)} %bitcast.49), calls=%async_computation.1 | async-start | bytes 8388608

commit v2 on v0

v2 whole, which is shorter than its diff:
```python
import jax
import jax.numpy as jnp
from jax import lax
from jax.experimental import pallas as pl
from jax.experimental.pallas import tpu as pltpu
from jax.sharding import PartitionSpec as P

MESH = pl.DeviceIdType.MESH
LENGTH = 256
EPSILON = 1e-06
BF = jnp.bfloat16
F32 = jnp.float32
VMEM_LIMIT = 56 << 20
CHUNKS = 4
NT = (((1,), (1,)), ((), ()))


class Place:
    def __init__(self):
        w, d = lax.axis_index("wide"), lax.axis_index("depth")
        self.zl, self.x, self.c = w // 8, (w // 2) % 4, w % 2
        self.zh, self.y = d // 4, d % 4
        self.d = d

    def at(self, zl=None, x=None, c=None, zh=None, y=None):
        zl = self.zl if zl is None else zl
        x = self.x if x is None else x
        c = self.c if c is None else c
        zh = self.zh if zh is None else zh
        y = self.y if y is None else y
        return (zl * 8 + x * 2 + c, zh * 4 + y)

    def ys(self):
        return [(self.y + k) % 4 for k in (2, 1, 3)]

    def xs(self):
        return [(self.x + k) % 4 for k in (2, 1, 3)]

    def zls(self):
        return [(self.zl + k) % 4 for k in (2, 1, 3)]

    def to_features(self):
        return dict(
            zl=self.c * 2 + self.zh,
            x=self.y,
            c=1 - self.x % 2,
            zh=self.zl // 2,
            y=(self.zl % 2) * 2 + self.x // 2,
        )

    def to_owner(self):
        return dict(
            zl=self.zh * 2 + self.y // 2,
            x=(self.y % 2) * 2 + 1 - self.c,
            c=self.zl // 2,
            zh=self.zl % 2,
            y=self.x,
        )


class Copies:
    def __init__(self, send_sem, recv_sem):
        self.send_sem, self.recv_sem = send_sem, recv_sem
        self.used = 0
        self.sent = []

    def make(self, source, target, device):
        copy = pltpu.make_async_remote_copy(
            src_ref=source,
            dst_ref=target,
            send_sem=self.send_sem.at[self.used],
            recv_sem=self.recv_sem.at[self.used],
            device_id=device,
            device_id_type=MESH,
        )
        self.used += 1
        return copy

    def send(self, source, target, device):
        copy = self.make(source, target, device)
        copy.start()
        self.sent.append(copy)
        return copy

    def finish(self):
        for copy in self.sent:
            copy.wait_send()


def arrived(copies):
    for copy in copies:
        copy.wait_recv()


def greet(senders, targets):
    barrier = pltpu.get_barrier_semaphore()
    for device in senders:
        pl.semaphore_signal(barrier, inc=1, device_id=device, device_id_type=MESH)
    pl.semaphore_wait(barrier, len(targets))


def part(index, size):
    return pl.ds(pl.multiple_of(index * size, size), size)


def diagonal():
    return lax.broadcasted_iota(jnp.int32, (128, 128), 0) == lax.broadcasted_iota(jnp.int32, (128, 128), 1)


def to_column(row):
    eye = diagonal()
    pieces = [
        jnp.sum(
            jnp.where(eye, jnp.broadcast_to(row[:, k : k + 128], (128, 128)), 0.0), axis=1, keepdims=True
        )
        for k in range(0, row.shape[1], 128)
    ]
    return jnp.concatenate(pieces, axis=0)


def to_row(column):
    eye = diagonal()
    pieces = [
        jnp.sum(
            jnp.where(eye, jnp.broadcast_to(column[k : k + 128], (128, 128)), 0.0), axis=0, keepdims=True
        )
        for k in range(0, column.shape[0], 128)
    ]
    return jnp.concatenate(pieces, axis=1)


def kernel(
    attn_ref, resid_ref, proj_ref, sec_ref, book_ref, dec_ref, head_ref, codes_ref,
    loss_ref, out_ref,
    wd, resid_part, full, pre, mine, sect, decs, book, head, embed, proj_in, logits, dlogits,
    to_scan, got, done, states, carry_in, carry_out,
    gsend, ggot, far_out, far_in, inners, gp, core_got, group, group_got, line, line_got, last,
    send_sem, recv_sem, local_sem,
):
    me = Place()
    copies = Copies(send_sem, recv_sem)
    frames, width = attn_ref.shape
    block = proj_ref.shape[0]
    inner_width = sec_ref.shape[1]
    chunk = inner_width // CHUNKS
    code_count = book.shape[0]
    rows = frames // 4
    half_frames = frames // 2

    local = [
        pltpu.make_async_copy(resid_ref.at[:, part(me.d, width)], resid_part, local_sem.at[0]),
        pltpu.make_async_copy(book_ref, book, local_sem.at[1]),
        pltpu.make_async_copy(head_ref, head, local_sem.at[2]),
    ]
    for copy in local:
        copy.start()
    carry_in[...] = jnp.zeros_like(carry_in)
    decs[me.y] = jnp.broadcast_to(dec_ref[...], decs.shape[1:])
    for j in range(CHUNKS):
        sect[j, me.zl, me.x, me.c] = sec_ref[:, j * chunk : (j + 1) * chunk]
    full[:, part(me.d, width)] = attn_ref[...]

    y_peers = [me.at(y=y) for y in me.ys()]
    x_peers = [me.at(x=x) for x in me.xs()]
    zl_peers = [me.at(zl=zl) for zl in me.zls()]
    right, left = me.at(x=(me.x + 1) % 4), me.at(x=(me.x + 3) % 4)
    far, other = me.at(zh=1 - me.zh), me.at(c=1 - me.c)
    cross = [me.at(zh=1 - me.zh, y=y) for y in me.ys()]
    there, home = me.to_features(), me.to_owner()
    shared = y_peers + x_peers + zl_peers + cross + [far, other]
    both = shared + [me.at(**there), me.at(**home)]
    greet(both, both)

    def gather_depth(buffer, source):
        own = buffer.at[:, part(me.d, width)]
        halves = []
        for k in range(2):
            place = buffer.at[pl.ds(k * half_frames, half_frames), part(me.d, width)]
            halves.append(copies.send(source.at[pl.ds(k * half_frames, half_frames)], place, far))
        near = [copies.send(source, own, peer) for peer in y_peers]

        def onward():
            sent = []
            for k in range(2):
                halves[k].wait_recv()
                place = buffer.at[
                    pl.ds(k * half_frames, half_frames), part((1 - me.zh) * 4 + me.y, width)
                ]
                sent += [copies.send(place, place, peer) for peer in y_peers]
            return sent

        return near, onward

    class Ring:
        def __init__(self, slot, view):
            self.slot, self.view = slot, view
            self.cores = []

        def line(self):
            self.zs = [copies.send(self.slot, self.slot, peer) for peer in zl_peers]

        def first(self):
            arrived(self.zs)
            group = self.view(me.x)
            self.right = copies.send(group, group, right)
            self.left = copies.send(group, group, left)
            self.cores.append(copies.send(group, group, other))

        def second(self):
            self.right.wait_recv()
            x = (me.x + 3) % 4
            self.on_right = copies.send(self.view(x, 0), self.view(x, 0), right)
            self.cores.append(copies.send(self.view(x), self.view(x), other))
            self.left.wait_recv()
            x = (me.x + 1) % 4
            self.on_left = copies.send(self.view(x, 1), self.view(x, 1), left)
            self.cores.append(copies.send(self.view(x), self.view(x), other))

        def third(self):
            arrived([self.on_right, self.on_left])
            group = self.view((me.x + 2) % 4)
            self.cores.append(copies.send(group, group, other))

        def end(self):
            arrived(self.cores)

    def wd_view(x, half=None):
        return wd.at[me.c, x] if half is None else wd.at[me.c, x, half]

    def sect_view(j):
        def view(x, half=None):
            return sect.at[j, :, x, me.c] if half is None else sect.at[j, pl.ds(2 * half, 2), x, me.c]

        return view

    wd_ring = Ring(wd.at[me.c, me.x, me.zl % 2, me.zl // 2], wd_view)
    sec_rings = [Ring(sect.at[j, me.zl, me.x, me.c], sect_view(j)) for j in range(CHUNKS)]

    moved = copies.send(
        proj_ref, wd.at[there["c"], there["x"], there["zl"] % 2, there["zl"] // 2], me.at(**there)
    )
    attn_near, attn_onward = gather_depth(full, attn_ref)
    dec_near = [copies.send(decs.at[me.y], decs.at[me.y], peer) for peer in y_peers]
    sec_rings[0].line()
    moved.wait_recv()
    wd_ring.line()
    sec_rings[0].first()
    attn_near += attn_onward()
    sec_rings[0].second()
    wd_ring.first()
    sec_rings[1].line()

    codes = codes_ref[...].astype(F32)
    code_rows = lax.broadcasted_iota(jnp.int32, codes.shape, 0)
    lanes = lax.broadcasted_iota(jnp.int32, (1, frames), 1)
    target = to_column(jnp.sum(jnp.where(code_rows == me.d, codes, 0.0), axis=0, keepdims=True))
    before = jnp.sum(jnp.where(code_rows == me.d - 1, codes, 0.0), axis=0, keepdims=True)
    shifted = pltpu.roll(codes, 1, 1)[codes.shape[0] - 1 :]
    shifted = jnp.where(lanes % LENGTH == 0, -1.0, shifted)
    previous = to_column(jnp.where(me.d == 0, shifted, before))
    code_lanes = lax.broadcasted_iota(jnp.int32, (frames, code_count), 1).astype(F32)
    for copy in local:
        copy.wait()
    embed[...] = jnp.dot(
        jnp.where(code_lanes == previous, 1.0, 0.0).astype(BF), book[...], preferred_element_type=F32
    )

    wd_ring.second()
    sec_rings[1].first()
    sec_rings[2].line()
    sec_rings[0].third()
    wd_ring.third()
    wd_ring.end()
    arrived(attn_near)

    for u in range(2):
        total = jnp.zeros((frames, 2 * block), F32)
        for h in range(8):
            weight = wd[1 - u, h % 4, h // 4].reshape(2 * block, width)
            total += lax.dot_general(
                full[:, h * width : (h + 1) * width], weight, NT, preferred_element_type=F32
            )
        features = pl.ds(u * 2 * block, 2 * block)
        mine[:, features] = (resid_part[:, features].astype(F32) + total).astype(BF)
    pre[:, part(me.d, width)] = mine[...]
    pre_near, pre_onward = gather_depth(pre, mine)

    sec_rings[1].second()
    sec_rings[2].first()
    sec_rings[3].line()
    sec_rings[1].third()
    sec_rings[2].second()
    sec_rings[3].first()
    pre_far_near = pre_onward()
    sec_rings[2].third()
    sec_rings[3].second()

    def squares(zh):
        value = jnp.zeros((frames, 1), F32)
        for y in range(4):
            piece = pre[:, part(zh * 4 + y, width)].astype(F32)
            value += jnp.sum(piece * piece, axis=1, keepdims=True)
        return value

    arrived(pre_near)
    mean = squares(me.zh)
    sec_rings[3].third()
    arrived(pre_far_near + dec_near)
    mean += squares(1 - me.zh)
    factor = lax.rsqrt(mean * (1.0 / pre.shape[1]) + EPSILON)

    def exchange(backward, value):
        way = 1 if backward else 0
        first = 1 if backward else 0
        sent = []
        for j in range(CHUNKS):
            to_scan[way, j] = value(j).astype(BF)
            sent.append(
                [copies.send(to_scan.at[way, j, part(y, rows)], got.at[way, j, me.y], me.at(y=y)) for y in me.ys()]
            )
            got[way, j, me.y] = to_scan[way, j, part(me.y, rows)]
        returned, carries = [], []
        for j in range(CHUNKS):
            arrived(sent[j])
            carry = copies.make(carry_out.at[way, j], carry_in.at[way, j], far)
            carries.append(carry)

            @pl.when(me.zh != first)
            def _(carry=carry):
                carry.wait_recv()

            state = carry_in[way, j].astype(F32)
            for section in reversed(range(4)) if backward else range(4):
                decay = decs[section, 0:1, j * chunk : (j + 1) * chunk]
                if backward:
                    here = got[way, j, section].astype(F32) + state
                    done[way, j, section] = here.astype(BF)
                    state = decay * here
                else:
                    state = decay * state + got[way, j, section].astype(F32)
                    done[way, j, section] = state.astype(BF)
            carry_out[way, j] = state.astype(BF)

            @pl.when(me.zh == first)
            def _(carry=carry):
                carry.start()

            returned.append(
                [copies.send(done.at[way, j, y], states.at[way, j, part(me.y, rows)], me.at(y=y)) for y in me.ys()]
            )
            states[way, j, part(me.y, rows)] = done[way, j, me.y]
        return returned, carries, first

    def entering(j):
        sec_rings[j].end()
        value = jnp.dot(
            pre[...], sect[j].reshape(pre.shape[1], chunk), preferred_element_type=F32
        )
        proj_in[j] = value
        return value * factor + embed[:, j * chunk : (j + 1) * chunk]

    returned, carries, first = exchange(False, entering)

    mean = jnp.zeros((frames, 1), F32)
    for j in range(CHUNKS):
        arrived(returned[j])
        value = states[0, j]
        wide = value.astype(F32)
        mean += jnp.sum(wide * wide, axis=1, keepdims=True)
        term = jnp.dot(value, head[j * chunk : (j + 1) * chunk], preferred_element_type=F32)
        logits[...] = term if j == 0 else logits[...] + term
    norm = lax.rsqrt(mean * (1.0 / inner_width) + EPSILON)
    loss_parts, inner_parts = [], []
    step = 64
    for start in range(0, frames, step):
        piece = pl.ds(start, step)
        value = logits[piece] * norm[start : start + step]
        chosen = lax.broadcasted_iota(jnp.int32, (step, code_count), 1).astype(F32) == target[start : start + step]
        top = jnp.max(value, axis=1, keepdims=True)
        raised = jnp.exp(value - top)
        total = jnp.sum(raised, axis=1, keepdims=True)
        picked = jnp.sum(jnp.where(chosen, value, 0.0), axis=1, keepdims=True)
        loss_parts.append(top + jnp.log(total) - picked)
        slope = (raised * (1.0 / total) - jnp.where(chosen, 1.0, 0.0)).astype(BF)
        dlogits[piece] = slope
        inner_parts.append(jnp.sum(slope.astype(F32) * value, axis=1, keepdims=True))
    loss_ref[...] = to_row(jnp.concatenate(loss_parts, axis=0))
    inner = jnp.concatenate(inner_parts, axis=0) * (1.0 / inner_width)

    def leaving(j):
        value = lax.dot_general(
            dlogits[...], head[j * chunk : (j + 1) * chunk], NT, preferred_element_type=F32
        )
        return norm * (value - states[0, j].astype(F32) * (norm * inner))

    returned, more, last_first = exchange(True, leaving)

    inner = jnp.zeros((frames, 1), F32)
    for j in range(CHUNKS):
        arrived(returned[j])
        inner += jnp.sum(states[1, j].astype(F32) * proj_in[j], axis=1, keepdims=True)
    inners[me.d] = jnp.broadcast_to(to_row(inner), inners.shape[1:])

    def term(u, zh, y):
        d = zh * 4 + y
        total = jnp.zeros((frames, 2 * block), F32)
        for j in range(CHUNKS):
            weight = sect[j, d // 2, (d % 2) * 2 + u].reshape(2 * block, chunk)
            total += lax.dot_general(states[1, j], weight, NT, preferred_element_type=F32)
        return total

    sums, kept = [], []
    for u in range(2):
        for k, zh in enumerate((1 - me.zh, me.zh)):
            sent = []
            for slot, y in enumerate(me.ys()):
                gsend[u, k, slot] = term(u, zh, y).astype(BF)
                sent.append(copies.send(gsend.at[u, k, slot], ggot.at[u, k, slot], me.at(y=y)))
            sums.append(sent)
            kept.append(term(u, zh, me.y))
        if u == 0:
            inner_sent = [copies.send(inners.at[me.d], inners.at[me.d], peer) for peer in y_peers + [far] + cross]

    order = me.xs() + [me.x]
    line_order = me.zls() + [me.zl]
    along = [
        [copies.make(group.at[x, zl], group_got.at[slot, k], me.at(x=x)) for k, zl in enumerate(line_order)]
        for slot, x in enumerate(order[:3])
    ]
    in_core = [[copies.make(gp.at[u, x], core_got.at[x], other) for x in order] for u in range(2)]
    crossing = []
    for u in range(2):
        total = kept[2 * u]
        for slot, copy in enumerate(sums[2 * u]):
            copy.wait_recv()
            total += ggot[u, 0, slot].astype(F32)
        far_out[u] = total.astype(BF)
        crossing.append(copies.send(far_out.at[u], far_in.at[u], far))
        total = kept[2 * u + 1]
        for slot, copy in enumerate(sums[2 * u + 1]):
            copy.wait_recv()
            total += ggot[u, 1, slot].astype(F32)
        if u == 0:
            arrived(inner_sent)
            inner = to_column(jnp.sum(inners[...], axis=0)[0:1])
            scale = factor * factor * factor * inner * (1.0 / pre.shape[1])
        crossing[u].wait_recv()
        total += far_in[u].astype(F32)
        dpre = factor * total - mine[:, u * 2 * block : (u + 1) * 2 * block].astype(F32) * scale
        turned = dpre.T.astype(BF)

        for slot, x in enumerate(order):
            for zh in range(2):
                value = jnp.dot(turned, full[:, part(zh * 4 + x, width)], preferred_element_type=F32).astype(BF)
                gp[u, x, zh] = value[:block]
                gp[u, x, 2 + zh] = value[block:]

            @pl.when(me.c == u)
            def _(copy=in_core[u][slot]):
                copy.start()

        @pl.when(me.c != u)
        def _(u=u):
            for slot, x in enumerate(order):
                in_core[u][slot].wait_recv()
                for k, zl in enumerate(line_order):
                    group[x, zl] = (gp[u, x, zl].astype(F32) + core_got[x, zl].astype(F32)).astype(BF)
                    if slot < 3:
                        along[slot][k].start()

    lines = []
    for k, zl in enumerate(line_order):
        value = group[me.x, zl].astype(F32)
        for slot in range(3):
            along[slot][k].wait_recv()
            value += group_got[slot, k].astype(F32)
        if k < 3:
            line[k] = value.astype(BF)
            lines.append(copies.send(line.at[k], line_got.at[k], me.at(zl=zl)))
    for k, copy in enumerate(lines):
        copy.wait_recv()
        value += line_got[k].astype(F32)
    last[...] = value.astype(BF)
    ending = copies.send(last, out_ref, me.at(**home))
    for u in range(2):

        @pl.when(me.c == u)
        def _(u=u):
            for copy in in_core[u]:
                copy.wait_send()

    for copies_of_slot in along:
        for copy in copies_of_slot:
            copy.wait_send()
    for made, start_at in ((carries, first), (more, last_first)):

        @pl.when(me.zh == start_at)
        def _(made=made):
            for copy in made:
                copy.wait_send()

    copies.finish()
    ending.wait_recv()


def local(attn_out, resid, out_proj, section_in, codebook, decays, section_out, codes):
    frames, width = attn_out.shape
    block = out_proj.shape[0]
    _, rows_in, inner = section_in.shape
    code_count = codebook.shape[1]
    chunk = inner // CHUNKS
    rows = frames // 4
    vmem = pl.BlockSpec(memory_space=pltpu.VMEM)
    anywhere = pl.BlockSpec(memory_space=pl.ANY)
    copies = 224
    return pl.pallas_call(
        kernel,
        out_shape=(
            jax.ShapeDtypeStruct((1, frames), F32),
            jax.ShapeDtypeStruct((block, width), BF),
        ),
        in_specs=[vmem, anywhere, vmem, vmem, anywhere, vmem, anywhere, vmem],
        out_specs=[vmem, vmem],
        scratch_shapes=[
            pltpu.VMEM((2, 4, 2, 2, block, width), BF),
            pltpu.VMEM((frames, width), BF),
            pltpu.VMEM((frames, 8 * width), BF),
            pltpu.VMEM((frames, 8 * width), BF),
            pltpu.VMEM((frames, width), BF),
            pltpu.VMEM((CHUNKS, 4, 4, 2, rows_in, chunk), BF),
            pltpu.VMEM((4, 8, inner), F32),
            pltpu.VMEM((code_count, inner), BF),
            pltpu.VMEM((inner, code_count), BF),
            pltpu.VMEM((frames, inner), F32),
            pltpu.VMEM((CHUNKS, frames, chunk), F32),
            pltpu.VMEM((frames, code_count), F32),
            pltpu.VMEM((frames, code_count), BF),
            pltpu.VMEM((2, CHUNKS, frames, chunk), BF),
            pltpu.VMEM((2, CHUNKS, 4, rows, chunk), BF),
            pltpu.VMEM((2, CHUNKS, 4, rows, chunk), BF),
            pltpu.VMEM((2, CHUNKS, frames, chunk), BF),
            pltpu.VMEM((2, CHUNKS, rows, chunk), BF),
            pltpu.VMEM((2, CHUNKS, rows, chunk), BF),
            pltpu.VMEM((2, 2, 3, frames, 2 * block), BF),
            pltpu.VMEM((2, 2, 3, frames, 2 * block), BF),
            pltpu.VMEM((2, frames, 2 * block), BF),
            pltpu.VMEM((2, frames, 2 * block), BF),
            pltpu.VMEM((8, 8, frames), F32),
            pltpu.VMEM((2, 4, 4, block, width), BF),
            pltpu.VMEM((4, 4, block, width), BF),
            pltpu.VMEM((4, 4, block, width), BF),
            pltpu.VMEM((3, 4, block, width), BF),
            pltpu.VMEM((3, block, width), BF),
            pltpu.VMEM((3, block, width), BF),
            pltpu.VMEM((block, width), BF),
            pltpu.SemaphoreType.DMA((copies,)),
            pltpu.SemaphoreType.DMA((copies,)),
            pltpu.SemaphoreType.DMA((3,)),
        ],
        compiler_params=pltpu.CompilerParams(
            collective_id=0, has_side_effects=True, vmem_limit_bytes=VMEM_LIMIT
        ),
        name="whole",
    )(attn_out, resid, out_proj, section_in[0], codebook[0], decays, section_out[0], codes)


def solution(mesh):
    return jax.shard_map(
        local,
        mesh=mesh,
        in_specs=(
            P("wide", "depth"),
            P("wide", None),
            P("wide", "depth"),
            P("depth", "wide", None),
            P("depth", None, None),
            P("depth", None),
            P("depth", None, None),
            P(None, "wide"),
        ),
        out_specs=(P("depth", "wide"), P("wide", "depth")),
        check_vma=False,
    )
```

time: 1110 us -> 207 us (0.19)
  the two profiles are of different devices: /device:TPU:27 before, /device:TPU:46 now
where the time goes in v2:
time: 207 us
  Pallas kernels  204 us (99%)
  local copies, waits for them, and re-layouts  2.8 us (1%)
    pallas_call x1, Pallas kernels, local(): pl.pallas_call(kernel, out_shape=(jax.ShapeDtypeStruct((1, frames), F32),...  204 us

profile of v2, /device:TPU:46, one launch (start us, length us, event | category | flops | bytes accessed | tf_op | source)
XLA Modules:
  0.0 207.3 jit_solution(396445434412912967)
XLA Ops:
  0.6 203.8 %whole.1 = (f32[1,256]{1,0:T(1,128)}, bf16[128,512]{1,0:T(8,128)(2,1)}) custom-call(bf16[256,512]{1,0:T(8,128)(2,1)} %attn_ref.1, bf16[256,4096]{1,0:T(8,128)(2,1)} %resid_ref.1, bf16[128,512]{1,0:T(8,128)(2,1)} %proj_ref.1, bf16[128,1024]{1,0:T(8,128)(2,1)} %bitcast.5, bf16[2048,1024]{1,0:T(8,128)(2,1)} %bitcast.3, f32[1,1024]{1,0:T(1,128)} %dec_ref.1, ...), custom_call_target="tpu_custom_call" | custom-call | tf_op jit(solution)/shard_map/whole/pallas_call | solution.py:516
  204.5 1.2 copy.12
  205.7 1.6 copy.13

commit v3 on v2

--- a/solution.py
+++ b/solution.py
@@ -41,9 +41,9 @@
 
     def to_features(self):
         return dict(
-            zl=self.c * 2 + self.zh,
+            zl=(self.x % 2) * 2 + self.zh,
             x=self.y,
-            c=1 - self.x % 2,
+            c=1 - self.c,
             zh=self.zl // 2,
             y=(self.zl % 2) * 2 + self.x // 2,
         )
@@ -51,8 +51,8 @@
     def to_owner(self):
         return dict(
             zl=self.zh * 2 + self.y // 2,
-            x=(self.y % 2) * 2 + 1 - self.c,
-            c=self.zl // 2,
+            x=(self.y % 2) * 2 + self.zl // 2,
+            c=1 - self.c,
             zh=self.zl % 2,
             y=self.x,
         )
@@ -132,10 +132,10 @@
 def kernel(
     attn_ref, resid_ref, proj_ref, sec_ref, book_ref, dec_ref, head_ref, codes_ref,
     loss_ref, out_ref,
-    wd, resid_part, full, pre, mine, sect, decs, book, head, embed, proj_in, logits, dlogits,
+    turned, wd, resid_part, full, pre, mine, sect, decs, book, head, embed, proj_in, logits, dlogits,
     to_scan, got, done, states, carry_in, carry_out,
     gsend, ggot, far_out, far_in, inners, gp, core_got, group, group_got, line, line_got, last,
-    send_sem, recv_sem, local_sem,
+    send_sem, recv_sem, local_sem, line_send, line_recv,
 ):
     me = Place()
     copies = Copies(send_sem, recv_sem)
@@ -172,24 +172,21 @@
     greet(both, both)
 
     def gather_depth(buffer, source):
-        own = buffer.at[:, part(me.d, width)]
         halves = []
         for k in range(2):
             place = buffer.at[pl.ds(k * half_frames, half_frames), part(me.d, width)]
             halves.append(copies.send(source.at[pl.ds(k * half_frames, half_frames)], place, far))
-        near = [copies.send(source, own, peer) for peer in y_peers]
-
-        def onward():
-            sent = []
-            for k in range(2):
-                halves[k].wait_recv()
-                place = buffer.at[
-                    pl.ds(k * half_frames, half_frames), part((1 - me.zh) * 4 + me.y, width)
-                ]
-                sent += [copies.send(place, place, peer) for peer in y_peers]
-            return sent
-
-        return near, onward
+
+        def onward(k):
+            halves[k].wait_recv()
+            place = buffer.at[pl.ds(k * half_frames, half_frames), part((1 - me.zh) * 4 + me.y, width)]
+            return [copies.send(place, place, peer) for peer in y_peers]
+
+        return onward
+
+    def gather_near(buffer, source):
+        own = buffer.at[:, part(me.d, width)]
+        return [copies.send(source, own, peer) for peer in y_peers]
 
     class Ring:
         def __init__(self, slot, view):
@@ -224,8 +221,16 @@
         def end(self):
             arrived(self.cores)
 
-    def wd_view(x, half=None):
-        return wd.at[me.c, x] if half is None else wd.at[me.c, x, half]
+    half_block = block // 2
+
+    def wd_view(k):
+        lines = pl.ds(k * half_block, half_block)
+
+        def view(x, half=None):
+            zls = slice(None) if half is None else pl.ds(2 * half, 2)
+            return wd.at[zls, x, 1 - me.c, lines]
+
+        return view
 
     def sect_view(j):
         def view(x, half=None):
@@ -233,22 +238,26 @@
 
         return view
 
-    wd_ring = Ring(wd.at[me.c, me.x, me.zl % 2, me.zl // 2], wd_view)
+    wd_rings = [
+        Ring(wd.at[me.zl, me.x, 1 - me.c, pl.ds(k * half_block, half_block)], wd_view(k))
+        for k in range(2)
+    ]
     sec_rings = [Ring(sect.at[j, me.zl, me.x, me.c], sect_view(j)) for j in range(CHUNKS)]
 
     moved = copies.send(
-        proj_ref, wd.at[there["c"], there["x"], there["zl"] % 2, there["zl"] // 2], me.at(**there)
+        proj_ref, wd.at[there["zl"], there["x"], 1 - there["c"]], me.at(**there)
     )
-    attn_near, attn_onward = gather_depth(full, attn_ref)
-    dec_near = [copies.send(decs.at[me.y], decs.at[me.y], peer) for peer in y_peers]
     sec_rings[0].line()
     moved.wait_recv()
-    wd_ring.line()
+    for ring in wd_rings:
+        ring.line()
+    attn_near = gather_near(full, attn_ref)
+    dec_near = [copies.send(decs.at[me.y], decs.at[me.y], peer) for peer in y_peers]
     sec_rings[0].first()
-    attn_near += attn_onward()
+    wd_rings[0].first()
+    attn_onward = gather_depth(full, attn_ref)
     sec_rings[0].second()
-    wd_ring.first()
-    sec_rings[1].line()
+    wd_rings[1].first()
 
     codes = codes_ref[...].astype(F32)
     code_rows = lax.broadcasted_iota(jnp.int32, codes.shape, 0)
@@ -265,46 +274,56 @@
         jnp.where(code_lanes == previous, 1.0, 0.0).astype(BF), book[...], preferred_element_type=F32
     )
 
-    wd_ring.second()
-    sec_rings[1].first()
+    sec_rings[1].line()
+    wd_rings[0].second()
+    attn_near += attn_onward(0)
+    wd_rings[1].second()
+    attn_near += attn_onward(1)
     sec_rings[2].line()
     sec_rings[0].third()
-    wd_ring.third()
-    wd_ring.end()
+    sec_rings[1].first()
+    wd_rings[0].third()
+    wd_rings[1].third()
+    for ring in wd_rings:
+        ring.end()
     arrived(attn_near)
 
     for u in range(2):
         total = jnp.zeros((frames, 2 * block), F32)
         for h in range(8):
-            weight = wd[1 - u, h % 4, h // 4].reshape(2 * block, width)
+            weight = wd[2 * u + h // 4, h % 4].reshape(2 * block, width)
             total += lax.dot_general(
                 full[:, h * width : (h + 1) * width], weight, NT, preferred_element_type=F32
             )
         features = pl.ds(u * 2 * block, 2 * block)
         mine[:, features] = (resid_part[:, features].astype(F32) + total).astype(BF)
     pre[:, part(me.d, width)] = mine[...]
-    pre_near, pre_onward = gather_depth(pre, mine)
+    pre_onward = gather_depth(pre, mine)
+    pre_near = gather_near(pre, mine)
+
+    def squares(zh):
+        value = pre[:, part(zh, 4 * width)].astype(F32)
+        return jnp.sum(value * value, axis=1, keepdims=True)
+
+    def projection(j, zh):
+        weight = sect[j, pl.ds(2 * zh, 2)].reshape(4 * width, chunk)
+        return jnp.dot(pre[:, part(zh, 4 * width)], weight, preferred_element_type=F32)
 
     sec_rings[1].second()
     sec_rings[2].first()
     sec_rings[3].line()
+    pre_far_near = pre_onward(0)
     sec_rings[1].third()
     sec_rings[2].second()
+    pre_far_near += pre_onward(1)
     sec_rings[3].first()
-    pre_far_near = pre_onward()
+    arrived(pre_near)
+    mean = squares(me.zh)
+    for j in range(2):
+        sec_rings[j].end()
+        proj_in[j] = projection(j, me.zh)
     sec_rings[2].third()
     sec_rings[3].second()
-
-    def squares(zh):
-        value = jnp.zeros((frames, 1), F32)
-        for y in range(4):
-            piece = pre[:, part(zh * 4 + y, width)].astype(F32)
-            value += jnp.sum(piece * piece, axis=1, keepdims=True)
-        return value
-
-    arrived(pre_near)
-    mean = squares(me.zh)
-    sec_rings[3].third()
     arrived(pre_far_near + dec_near)
     mean += squares(1 - me.zh)
     factor = lax.rsqrt(mean * (1.0 / pre.shape[1]) + EPSILON)
@@ -352,10 +371,12 @@
         return returned, carries, first
 
     def entering(j):
-        sec_rings[j].end()
-        value = jnp.dot(
-            pre[...], sect[j].reshape(pre.shape[1], chunk), preferred_element_type=F32
-        )
+        if j == 3:
+            sec_rings[3].third()
+        if j >= 2:
+            sec_rings[j].end()
+            proj_in[j] = projection(j, me.zh)
+        value = proj_in[j] + projection(j, 1 - me.zh)
         proj_in[j] = value
         return value * factor + embed[:, j * chunk : (j + 1) * chunk]
 
@@ -400,6 +421,7 @@
         arrived(returned[j])
         inner += jnp.sum(states[1, j].astype(F32) * proj_in[j], axis=1, keepdims=True)
     inners[me.d] = jnp.broadcast_to(to_row(inner), inners.shape[1:])
+    inner_sent = [copies.send(inners.at[me.d], inners.at[me.d], peer) for peer in y_peers + [far] + cross]
 
     def term(u, zh, y):
         d = zh * 4 + y
@@ -409,89 +431,132 @@
             total += lax.dot_general(states[1, j], weight, NT, preferred_element_type=F32)
         return total
 
-    sums, kept = [], []
+    sums, kept = {}, {}
+    order = me.xs() + [me.x]
     for u in range(2):
         for k, zh in enumerate((1 - me.zh, me.zh)):
-            sent = []
             for slot, y in enumerate(me.ys()):
-                gsend[u, k, slot] = term(u, zh, y).astype(BF)
-                sent.append(copies.send(gsend.at[u, k, slot], ggot.at[u, k, slot], me.at(y=y)))
-            sums.append(sent)
-            kept.append(term(u, zh, me.y))
-        if u == 0:
-            inner_sent = [copies.send(inners.at[me.d], inners.at[me.d], peer) for peer in y_peers + [far] + cross]
-
-    order = me.xs() + [me.x]
-    line_order = me.zls() + [me.zl]
+                value = term(u, zh, y).astype(BF)
+                for lo in range(2):
+                    gsend[2 * u + lo, k, slot] = value[:, lo * block : (lo + 1) * block]
+            kept[u, k] = term(u, zh, me.y)
+            sums[2 * u, k] = [
+                copies.send(gsend.at[2 * u, k, slot], ggot.at[2 * u, k, slot], me.at(y=y))
+                for slot, y in enumerate(me.ys())
+            ]
+        for k in range(2):
+            sums[2 * u + 1, k] = [
+                copies.send(gsend.at[2 * u + 1, k, slot], ggot.at[2 * u + 1, k, slot], me.at(y=y))
+                for slot, y in enumerate(me.ys())
+            ]
+
     along = [
-        [copies.make(group.at[x, zl], group_got.at[slot, k], me.at(x=x)) for k, zl in enumerate(line_order)]
-        for slot, x in enumerate(order[:3])
+        [
+            [copies.make(group.at[hi, x, zh], group_got.at[slot, hi, zh], me.at(x=x)) for zh in range(2)]
+            for slot, x in enumerate(order[:3])
+        ]
+        for hi in range(2)
     ]
-    in_core = [[copies.make(gp.at[u, x], core_got.at[x], other) for x in order] for u in range(2)]
-    crossing = []
-    for u in range(2):
-        total = kept[2 * u]
-        for slot, copy in enumerate(sums[2 * u]):
+    in_core = [[copies.make(gp.at[q, x], core_got.at[q // 2, x], other) for x in order] for q in range(4)]
+
+    def reduced(q, k):
+        lo = q % 2
+        total = kept[q // 2, k][:, lo * block : (lo + 1) * block]
+        for slot, copy in enumerate(sums[q, k]):
             copy.wait_recv()
-            total += ggot[u, 0, slot].astype(F32)
-        far_out[u] = total.astype(BF)
-        crossing.append(copies.send(far_out.at[u], far_in.at[u], far))
-        total = kept[2 * u + 1]
-        for slot, copy in enumerate(sums[2 * u + 1]):
-            copy.wait_recv()
-            total += ggot[u, 1, slot].astype(F32)
-        if u == 0:
+            total += ggot[q, k, slot].astype(F32)
+        return total
+
+    def cross_part(q):
+        far_out[q] = reduced(q, 0).astype(BF)
+        return copies.send(far_out.at[q], far_in.at[q], far)
+
+    crossing = [cross_part(0)]
+    for q in range(4):
+        total = reduced(q, 1)
+        if q < 3:
+            crossing.append(cross_part(q + 1))
+        if q == 0:
             arrived(inner_sent)
             inner = to_column(jnp.sum(inners[...], axis=0)[0:1])
             scale = factor * factor * factor * inner * (1.0 / pre.shape[1])
-        crossing[u].wait_recv()
-        total += far_in[u].astype(F32)
-        dpre = factor * total - mine[:, u * 2 * block : (u + 1) * 2 * block].astype(F32) * scale
-        turned = dpre.T.astype(BF)
+        crossing[q].wait_recv()
+        total += far_in[q].astype(F32)
+        dpre = factor * total - mine[:, q * block : (q + 1) * block].astype(F32) * scale
+        turned[q] = dpre.T.astype(BF)
 
         for slot, x in enumerate(order):
             for zh in range(2):
-                value = jnp.dot(turned, full[:, part(zh * 4 + x, width)], preferred_element_type=F32).astype(BF)
-                gp[u, x, zh] = value[:block]
-                gp[u, x, 2 + zh] = value[block:]
-
-            @pl.when(me.c == u)
-            def _(copy=in_core[u][slot]):
+                gp[q, x, zh] = jnp.dot(
+                    turned[q], full[:, part(zh * 4 + x, width)], preferred_element_type=F32
+                ).astype(BF)
+
+            @pl.when(me.c == q % 2)
+            def _(copy=in_core[q][slot]):
                 copy.start()
 
-        @pl.when(me.c != u)
-        def _(u=u):
+        @pl.when(me.c != q % 2)
+        def _(q=q, hi=q // 2):
             for slot, x in enumerate(order):
-                in_core[u][slot].wait_recv()
-                for k, zl in enumerate(line_order):
-                    group[x, zl] = (gp[u, x, zl].astype(F32) + core_got[x, zl].astype(F32)).astype(BF)
+                in_core[q][slot].wait_recv()
+                for zh in range(2):
+                    group[hi, x, zh] = (gp[q, x, zh].astype(F32) + core_got[hi, x, zh].astype(F32)).astype(BF)
                     if slot < 3:
-                        along[slot][k].start()
-
-    lines = []
-    for k, zl in enumerate(line_order):
-        value = group[me.x, zl].astype(F32)
+                        along[hi][slot][zh].start()
+
+    def line_copy(zl):
+        return pltpu.make_async_remote_copy(
+            src_ref=line.at[zl],
+            dst_ref=line_got.at[me.zl],
+            send_sem=line_send.at[zl],
+            recv_sem=line_recv.at[me.zl],
+            device_id=me.at(zl=zl),
+            device_id_type=MESH,
+        )
+
+    for zl in range(4):
+        hi, zh = zl // 2, zl % 2
+        value = group[hi, me.x, zh].astype(F32)
         for slot in range(3):
-            along[slot][k].wait_recv()
-            value += group_got[slot, k].astype(F32)
-        if k < 3:
-            line[k] = value.astype(BF)
-            lines.append(copies.send(line.at[k], line_got.at[k], me.at(zl=zl)))
-    for k, copy in enumerate(lines):
-        copy.wait_recv()
-        value += line_got[k].astype(F32)
+            along[hi][slot][zh].wait_recv()
+            value += group_got[slot, hi, zh].astype(F32)
+        line[zl] = value.astype(BF)
+
+        @pl.when(me.zl != zl)
+        def _(zl=zl):
+            line_copy(zl).start()
+
+    value = line[me.zl].astype(F32)
+    for k in range(1, 4):
+        zl = (me.zl + k) % 4
+        pltpu.make_async_remote_copy(
+            src_ref=line.at[zl],
+            dst_ref=line_got.at[zl],
+            send_sem=line_send.at[zl],
+            recv_sem=line_recv.at[zl],
+            device_id=me.at(zl=zl),
+            device_id_type=MESH,
+        ).wait_recv()
+        value += line_got[zl].astype(F32)
     last[...] = value.astype(BF)
     ending = copies.send(last, out_ref, me.at(**home))
-    for u in range(2):
-
-        @pl.when(me.c == u)
-        def _(u=u):
-            for copy in in_core[u]:
+    for zl in range(4):
+
+        @pl.when(me.zl != zl)
+        def _(zl=zl):
+            line_copy(zl).wait_send()
+
+    for q in range(4):
+
+        @pl.when(me.c == q % 2)
+        def _(q=q):
+            for copy in in_core[q]:
                 copy.wait_send()
 
-    for copies_of_slot in along:
-        for copy in copies_of_slot:
-            copy.wait_send()
+    for side in along:
+        for slot in side:
+            for copy in slot:
+                copy.wait_send()
     for made, start_at in ((carries, first), (more, last_first)):
 
         @pl.when(me.zh == start_at)
@@ -512,7 +577,7 @@
     rows = frames // 4
     vmem = pl.BlockSpec(memory_space=pltpu.VMEM)
     anywhere = pl.BlockSpec(memory_space=pl.ANY)
-    copies = 224
+    copies = 256
     return pl.pallas_call(
         kernel,
         out_shape=(
@@ -522,7 +587,8 @@
         in_specs=[vmem, anywhere, vmem, vmem, anywhere, vmem, anywhere, vmem],
         out_specs=[vmem, vmem],
         scratch_shapes=[
-            pltpu.VMEM((2, 4, 2, 2, block, width), BF),
+            pltpu.VMEM((4, block, frames), BF),
+            pltpu.VMEM((4, 4, 2, block, width), BF),
             pltpu.VMEM((frames, width), BF),
             pltpu.VMEM((frames, 8 * width), BF),
             pltpu.VMEM((frames, 8 * width), BF),
@@ -541,21 +607,23 @@
             pltpu.VMEM((2, CHUNKS, frames, chunk), BF),
             pltpu.VMEM((2, CHUNKS, rows, chunk), BF),
             pltpu.VMEM((2, CHUNKS, rows, chunk), BF),
-            pltpu.VMEM((2, 2, 3, frames, 2 * block), BF),
-            pltpu.VMEM((2, 2, 3, frames, 2 * block), BF),
-            pltpu.VMEM((2, frames, 2 * block), BF),
-            pltpu.VMEM((2, frames, 2 * block), BF),
+            pltpu.VMEM((4, 2, 3, frames, block), BF),
+            pltpu.VMEM((4, 2, 3, frames, block), BF),
+            pltpu.VMEM((4, frames, block), BF),
+            pltpu.VMEM((4, frames, block), BF),
             pltpu.VMEM((8, 8, frames), F32),
-            pltpu.VMEM((2, 4, 4, block, width), BF),
-            pltpu.VMEM((4, 4, block, width), BF),
-            pltpu.VMEM((4, 4, block, width), BF),
-            pltpu.VMEM((3, 4, block, width), BF),
-            pltpu.VMEM((3, block, width), BF),
-            pltpu.VMEM((3, block, width), BF),
+            pltpu.VMEM((4, 4, 2, block, width), BF),
+            pltpu.VMEM((2, 4, 2, block, width), BF),
+            pltpu.VMEM((2, 4, 2, block, width), BF),
+            pltpu.VMEM((3, 2, 2, block, width), BF),
+            pltpu.VMEM((4, block, width), BF),
+            pltpu.VMEM((4, block, width), BF),
             pltpu.VMEM((block, width), BF),
             pltpu.SemaphoreType.DMA((copies,)),
             pltpu.SemaphoreType.DMA((copies,)),
             pltpu.SemaphoreType.DMA((3,)),
+            pltpu.SemaphoreType.DMA((4,)),
+            pltpu.SemaphoreType.DMA((4,)),
         ],
         compiler_params=pltpu.CompilerParams(
             collective_id=0, has_side_effects=True, vmem_limit_bytes=VMEM_LIMIT

time: 207 us -> 197 us (0.952)
  the two profiles are of different devices: /device:TPU:46 before, /device:TPU:27 now
where the time goes in v3:
time: 197 us; the launch traced here: 195 us
  Pallas kernels  191 us (97%)
  local copies, waits for them, and re-layouts  2.8 us (1%)
    pallas_call x1, Pallas kernels, local(): pl.pallas_call(kernel, out_shape=(jax.ShapeDtypeStruct((1, frames), F32),...  191 us

profile of v3, /device:TPU:27, one launch (start us, length us, event | category | flops | bytes accessed | tf_op | source)
XLA Modules:
  0.0 194.7 jit_solution(13465139402855893738)
XLA Ops:
  0.6 191.3 %whole.1 = (f32[1,256]{1,0:T(1,128)}, bf16[128,512]{1,0:T(8,128)(2,1)}) custom-call(bf16[256,512]{1,0:T(8,128)(2,1)} %attn_ref.1, bf16[256,4096]{1,0:T(8,128)(2,1)} %resid_ref.1, bf16[128,512]{1,0:T(8,128)(2,1)} %proj_ref.1, bf16[128,1024]{1,0:T(8,128)(2,1)} %bitcast.5, bf16[2048,1024]{1,0:T(8,128)(2,1)} %bitcast.3, f32[1,1024]{1,0:T(1,128)} %dec_ref.1, ...), custom_call_target="tpu_custom_call" | custom-call | tf_op jit(solution)/shard_map/whole/pallas_call | solution.py:581
  191.9 1.2 copy.12
  193.2 1.6 copy.13

commit v4 on v3

--- a/solution.py
+++ b/solution.py
@@ -12,6 +12,7 @@
 F32 = jnp.float32
 VMEM_LIMIT = 56 << 20
 CHUNKS = 4
+PAIRS = ((0, 3), (1, 2))
 NT = (((1,), (1,)), ((), ()))
 
 
@@ -41,7 +42,7 @@
 
     def to_features(self):
         return dict(
-            zl=(self.x % 2) * 2 + self.zh,
+            zl=3 * self.zh + (self.x % 2) * (1 - 2 * self.zh),
             x=self.y,
             c=1 - self.c,
             zh=self.zl // 2,
@@ -51,9 +52,9 @@
     def to_owner(self):
         return dict(
             zl=self.zh * 2 + self.y // 2,
-            x=(self.y % 2) * 2 + self.zl // 2,
+            x=(self.y % 2) * 2 + ((self.zl + 1) // 2) % 2,
             c=1 - self.c,
-            zh=self.zl % 2,
+            zh=self.zl // 2,
             y=self.x,
         )
 
@@ -171,22 +172,26 @@
     both = shared + [me.at(**there), me.at(**home)]
     greet(both, both)
 
-    def gather_depth(buffer, source):
-        halves = []
-        for k in range(2):
-            place = buffer.at[pl.ds(k * half_frames, half_frames), part(me.d, width)]
-            halves.append(copies.send(source.at[pl.ds(k * half_frames, half_frames)], place, far))
-
-        def onward(k):
-            halves[k].wait_recv()
-            place = buffer.at[pl.ds(k * half_frames, half_frames), part((1 - me.zh) * 4 + me.y, width)]
-            return [copies.send(place, place, peer) for peer in y_peers]
-
-        return onward
-
-    def gather_near(buffer, source):
-        own = buffer.at[:, part(me.d, width)]
-        return [copies.send(source, own, peer) for peer in y_peers]
+    up, down = me.at(y=(me.y + 1) % 4), me.at(y=(me.y + 3) % 4)
+
+    def piece(buffer, zh, y, k):
+        return buffer.at[pl.ds(k * half_frames, half_frames), part(zh * 4 + y, width)]
+
+    def cross_over(buffer, source):
+        return [
+            copies.send(source.at[pl.ds(k * half_frames, half_frames)], piece(buffer, me.zh, me.y, k), far)
+            for k in range(2)
+        ]
+
+    def spread(buffer, zh, k, source=None):
+        place = piece(buffer, zh, me.y, k)
+        source = place if source is None else source.at[pl.ds(k * half_frames, half_frames)]
+        return copies.send(source, place, up), copies.send(source, place, down)
+
+    def forward(buffer, zh, k, pair):
+        pair[k].wait_recv()
+        place = piece(buffer, zh, (me.y + (3, 1)[k]) % 4, k)
+        return [copies.send(place, place, (up, down)[k]), pair[1 - k]]
 
     class Ring:
         def __init__(self, slot, view):
@@ -251,11 +256,14 @@
     moved.wait_recv()
     for ring in wd_rings:
         ring.line()
-    attn_near = gather_near(full, attn_ref)
+    attn_near = [spread(full, me.zh, k, attn_ref) for k in range(2)]
     dec_near = [copies.send(decs.at[me.y], decs.at[me.y], peer) for peer in y_peers]
     sec_rings[0].first()
     wd_rings[0].first()
-    attn_onward = gather_depth(full, attn_ref)
+    attn_cross = cross_over(full, attn_ref)
+    attn_done = []
+    for k in range(2):
+        attn_done += forward(full, me.zh, k, attn_near[k])
     sec_rings[0].second()
     wd_rings[1].first()
 
@@ -276,30 +284,35 @@
 
     sec_rings[1].line()
     wd_rings[0].second()
-    attn_near += attn_onward(0)
+    attn_far = []
+    for k in range(2):
+        attn_cross[k].wait_recv()
+        attn_far.append(spread(full, 1 - me.zh, k))
     wd_rings[1].second()
-    attn_near += attn_onward(1)
     sec_rings[2].line()
+    sec_rings[3].line()
     sec_rings[0].third()
+    attn_done += forward(full, 1 - me.zh, 0, attn_far[0])
+    wd_rings[0].third()
+    attn_done += forward(full, 1 - me.zh, 1, attn_far[1])
+    wd_rings[1].third()
     sec_rings[1].first()
-    wd_rings[0].third()
-    wd_rings[1].third()
     for ring in wd_rings:
         ring.end()
-    arrived(attn_near)
+    arrived(attn_done)
 
     for u in range(2):
         total = jnp.zeros((frames, 2 * block), F32)
         for h in range(8):
-            weight = wd[2 * u + h // 4, h % 4].reshape(2 * block, width)
+            weight = wd[PAIRS[u][h // 4], h % 4].reshape(2 * block, width)
             total += lax.dot_general(
                 full[:, h * width : (h + 1) * width], weight, NT, preferred_element_type=F32
             )
         features = pl.ds(u * 2 * block, 2 * block)
         mine[:, features] = (resid_part[:, features].astype(F32) + total).astype(BF)
     pre[:, part(me.d, width)] = mine[...]
-    pre_onward = gather_depth(pre, mine)
-    pre_near = gather_near(pre, mine)
+    pre_cross = cross_over(pre, mine)
+    pre_near = [spread(pre, me.zh, k, mine) for k in range(2)]
 
     def squares(zh):
         value = pre[:, part(zh, 4 * width)].astype(F32)
@@ -311,20 +324,26 @@
 
     sec_rings[1].second()
     sec_rings[2].first()
-    sec_rings[3].line()
-    pre_far_near = pre_onward(0)
+    sec_rings[3].first()
+    pre_near_done, pre_far, pre_far_done = [], [], []
+    for k in range(2):
+        pre_near_done += forward(pre, me.zh, k, pre_near[k])
+    pre_cross[0].wait_recv()
+    pre_far.append(spread(pre, 1 - me.zh, 0))
     sec_rings[1].third()
     sec_rings[2].second()
-    pre_far_near += pre_onward(1)
-    sec_rings[3].first()
-    arrived(pre_near)
+    pre_cross[1].wait_recv()
+    pre_far.append(spread(pre, 1 - me.zh, 1))
+    sec_rings[2].third()
+    sec_rings[3].second()
+    for k in range(2):
+        pre_far_done += forward(pre, 1 - me.zh, k, pre_far[k])
+    arrived(pre_near_done)
     mean = squares(me.zh)
-    for j in range(2):
+    for j in range(3):
         sec_rings[j].end()
         proj_in[j] = projection(j, me.zh)
-    sec_rings[2].third()
-    sec_rings[3].second()
-    arrived(pre_far_near + dec_near)
+    arrived(pre_far_done + dec_near)
     mean += squares(1 - me.zh)
     factor = lax.rsqrt(mean * (1.0 / pre.shape[1]) + EPSILON)
 
@@ -373,8 +392,7 @@
     def entering(j):
         if j == 3:
             sec_rings[3].third()
-        if j >= 2:
-            sec_rings[j].end()
+            sec_rings[3].end()
             proj_in[j] = projection(j, me.zh)
         value = proj_in[j] + projection(j, 1 - me.zh)
         proj_in[j] = value
@@ -514,8 +532,8 @@
             device_id_type=MESH,
         )
 
-    for zl in range(4):
-        hi, zh = zl // 2, zl % 2
+    for hi, zh in ((0, 0), (0, 1), (1, 0), (1, 1)):
+        zl = PAIRS[hi][zh]
         value = group[hi, me.x, zh].astype(F32)
         for slot in range(3):
             along[hi][slot][zh].wait_recv()

time: 197 us -> 189 us (0.959); the launches traced: 195 us -> 189 us
  Pallas kernels: 191 us -> 186 us
    pallas_call x1, Pallas kernels: 191 us -> 186 us  [local(): pl.pallas_call(kernel, out_shape=(jax.ShapeDtypeStruct((1, frames), F32),...]
where the time goes in v4:
time: 189 us
  Pallas kernels  186 us (98%)
  local copies, waits for them, and re-layouts  2.8 us (1%)
    pallas_call x1, Pallas kernels, local(): pl.pallas_call(kernel, out_shape=(jax.ShapeDtypeStruct((1, frames), F32),...  186 us

profile of v4, /device:TPU:27, one launch (start us, length us, event | category | flops | bytes accessed | tf_op | source)
XLA Modules:
  0.0 189.3 jit_solution(10440423309735617255)
XLA Ops:
  0.6 185.9 %whole.1 = (f32[1,256]{1,0:T(1,128)}, bf16[128,512]{1,0:T(8,128)(2,1)}) custom-call(bf16[256,512]{1,0:T(8,128)(2,1)} %attn_ref.1, bf16[256,4096]{1,0:T(8,128)(2,1)} %resid_ref.1, bf16[128,512]{1,0:T(8,128)(2,1)} %proj_ref.1, bf16[128,1024]{1,0:T(8,128)(2,1)} %bitcast.5, bf16[2048,1024]{1,0:T(8,128)(2,1)} %bitcast.3, f32[1,1024]{1,0:T(1,128)} %dec_ref.1, ...), custom_call_target="tpu_custom_call" | custom-call | tf_op jit(solution)/shard_map/whole/pallas_call | solution.py:599
  186.5 1.2 copy.12
  187.7 1.6 copy.13

commit v5 on v4

--- a/solution.py
+++ b/solution.py
@@ -410,7 +410,7 @@
         logits[...] = term if j == 0 else logits[...] + term
     norm = lax.rsqrt(mean * (1.0 / inner_width) + EPSILON)
     loss_parts, inner_parts = [], []
-    step = 64
+    step = 128
     for start in range(0, frames, step):
         piece = pl.ds(start, step)
         value = logits[piece] * norm[start : start + step]

time: 189 us -> 189 us (level)
  no operation moved by 1% of the time
where the time goes in v5:
time: 189 us
  Pallas kernels  186 us (98%)
  local copies, waits for them, and re-layouts  2.8 us (1%)
    pallas_call x1, Pallas kernels, local(): pl.pallas_call(kernel, out_shape=(jax.ShapeDtypeStruct((1, frames), F32),...  186 us

profile of v5, /device:TPU:27, one launch (start us, length us, event | category | flops | bytes accessed | tf_op | source)
XLA Modules:
  0.0 189.3 jit_solution(10440423309735617255)
XLA Ops:
  0.6 185.9 %whole.1 = (f32[1,256]{1,0:T(1,128)}, bf16[128,512]{1,0:T(8,128)(2,1)}) custom-call(bf16[256,512]{1,0:T(8,128)(2,1)} %attn_ref.1, bf16[256,4096]{1,0:T(8,128)(2,1)} %resid_ref.1, bf16[128,512]{1,0:T(8,128)(2,1)} %proj_ref.1, bf16[128,1024]{1,0:T(8,128)(2,1)} %bitcast.5, bf16[2048,1024]{1,0:T(8,128)(2,1)} %bitcast.3, f32[1,1024]{1,0:T(1,128)} %dec_ref.1, ...), custom_call_target="tpu_custom_call" | custom-call | tf_op jit(solution)/shard_map/whole/pallas_call | solution.py:599
  186.5 1.2 copy.12
  187.7 1.6 copy.13
